TPU v7x, 512 devices: a whole 4x8x8 slice. The times are simulated.
512 devices in a mesh: attn: 8 (over x, core), tp: 8 (over z), exp: 8 (over y).
Axes of the slice: x: 4, y: 8, z: 8, core: 2. Of those that a mesh axis runs over, the one named last changes fastest.
Arguments:
- queries: bfloat16 [1536, 3072], P(('attn', 'exp'), 'tp'), may hold values from -180 to 180
- key_cache: bfloat16 [1536, 8, 32, 128], P(('attn', 'exp'), 'tp'), may hold values from -6 to 6
- value_cache: bfloat16 [1536, 8, 32, 128], P(('attn', 'exp'), 'tp'), may hold values from -6 to 6
- new_key: bfloat16 [1536, 1024], P(('attn', 'exp'), 'tp'), may hold values from -8 to 8
- new_value: bfloat16 [1536, 1024], P(('attn', 'exp'), 'tp'), may hold values from -6 to 6
- lengths: int32 [1536], P(('attn', 'exp')), may hold values from 2 to 32, as said below
- residual: bfloat16 [1536, 3072], P(('attn', 'exp'), 'tp'), may hold values from -150 to 150
- norm_gain: float32 [3072], replicated, may hold values from 0.1 to 1.9
- routes: int32 [1536, 2], P(('attn', 'exp')), may hold values from 0 to 7, all different within a row; in each aligned block of 24 rows (0 to 23, 24 to 47, ...) at most 12 rows name the same one
- route_weights: float32 [1536, 2], P(('attn', 'exp')), may hold values from 0.1 to 1
- w_gate_up: bfloat16 [8, 3072, 2, 16384], P('exp', None, None, ('attn', 'tp')), may hold values from -0.109375 to 0.109375
- w_down: bfloat16 [8, 16384, 3072], P('exp', 'attn', 'tp'), may hold values from -0.046875 to 0.046875
Outputs:
- attn_out: bfloat16 [1536, 3072], P(('attn', 'exp'), 'tp')
- moe_out: bfloat16 [1536, 3072], P(('attn', 'exp'), 'tp')
Inputs may be any that keep to these rules, and one draw needn't show every extreme that they name: `lengths`: at least 2; some row holds exactly 32. `routes`: each row names two different experts; in the rows of one attention replica (aligned blocks of 24 rows) no expert is named by more than 12 rows, and in some block an expert is named by exactly 12 rows.
All inputs are finite; a program needn't handle non-finite values.
Results may differ from a plain program's by a relative error of at most 0.022.
Values may be sent and summed in bfloat16 or wider, within the bound.
No kernel may reach another device: no remote copies, remote signals or barrier semaphores. Data moves between devices by JAX's collectives and lax.ppermute only.
A program may use at most 64 MiB of HBM per device.

v0:
```python
import math

import jax
import jax.numpy as jnp
from jax import lax
from jax.sharding import PartitionSpec as P

HD = 128
EXPERTS = 8


def attend_local(queries, key_cache, value_cache, new_key, new_value, lengths):
    row_count = key_cache.shape[0]
    kv_local = key_cache.shape[1]
    query_heads = queries.reshape(row_count, kv_local, -1, HD)
    fresh_key = new_key.reshape(row_count, kv_local, HD)
    fresh_value = new_value.reshape(row_count, kv_local, HD)
    score_scale = 1.0 / math.sqrt(HD)
    scores = (
        jnp.einsum("rkgd,rkpd->rkgp", query_heads, key_cache, preferred_element_type=jnp.float32)
        * score_scale
    )
    own_score = (
        jnp.einsum("rkgd,rkd->rkg", query_heads, fresh_key, preferred_element_type=jnp.float32)
        * score_scale
    )
    valid = (
        jnp.arange(key_cache.shape[2], dtype=jnp.int32)[None, None, None, :]
        < lengths[:, None, None, None]
    )
    masked = jnp.where(valid, scores, -jnp.inf)
    row_max = jnp.maximum(jnp.max(masked, axis=-1), own_score)
    exp_terms = jnp.exp(masked - row_max[..., None])
    own_term = jnp.exp(own_score - row_max)
    denominator = jnp.sum(exp_terms, axis=-1) + own_term
    probs = (exp_terms / denominator[..., None]).astype(jnp.bfloat16)
    probs_new = (own_term / denominator).astype(jnp.bfloat16)
    attended = jnp.einsum("rkgp,rkpd->rkgd", probs, value_cache, preferred_element_type=jnp.float32)
    attended = (
        attended
        + probs_new.astype(jnp.float32)[..., None] * fresh_value.astype(jnp.float32)[:, :, None, :]
    )
    return attended.reshape(row_count, -1).astype(jnp.bfloat16)


def slots_of(block_routes):
    flat_routes = block_routes.reshape(-1)
    onehot = (flat_routes[:, None] == jnp.arange(EXPERTS, dtype=jnp.int32)[None, :]).astype(
        jnp.int32
    )
    before = jnp.cumsum(onehot, axis=0) - onehot
    return jnp.sum(before * onehot, axis=1).reshape(block_routes.shape)


def body(
    queries,
    key_cache,
    value_cache,
    new_key,
    new_value,
    lengths,
    residual,
    norm_gain,
    routes,
    route_weights,
    w_gate_up,
    w_down,
):
    attn_out = attend_local(queries, key_cache, value_cache, new_key, new_value, lengths)
    hidden_part = (residual.astype(jnp.float32) + attn_out.astype(jnp.float32)).astype(jnp.bfloat16)
    hidden = lax.all_gather(hidden_part, "tp", axis=1, tiled=True)
    hidden_wide = hidden.astype(jnp.float32)
    inv_rms = lax.rsqrt(jnp.mean(hidden_wide * hidden_wide, axis=1, keepdims=True) + 1e-05)
    normed = (hidden_wide * inv_rms * norm_gain[None, :]).astype(jnp.bfloat16)
    row_count = queries.shape[0]
    capacity = row_count // 2
    slot_total = EXPERTS * capacity
    feature_count = normed.shape[1]
    local_experts = w_gate_up.shape[0]
    n_attn = lax.axis_size("attn")
    n_exp = lax.axis_size("exp")
    target = routes * capacity + slots_of(routes)
    slot_ids = jnp.arange(slot_total, dtype=jnp.int32)
    placement = jnp.any(slot_ids[:, None, None] == target[None, :, :], axis=2).astype(jnp.bfloat16)
    packed = jnp.dot(placement, normed, preferred_element_type=jnp.float32).astype(jnp.bfloat16)
    packed = packed.reshape(n_exp, local_experts * capacity, feature_count)
    spread = jnp.broadcast_to(packed[None], (n_attn,) + packed.shape)
    spread = spread.reshape(n_attn * n_exp, local_experts * capacity, feature_count)
    arrived = lax.all_to_all(spread, ("attn", "exp"), split_axis=0, concat_axis=0, tiled=True)
    incoming = arrived.reshape(n_attn, n_exp, local_experts * capacity, feature_count)
    blocks = incoming.reshape(
        incoming.shape[0], incoming.shape[1], local_experts, capacity, feature_count
    )
    pre_act = jnp.einsum(
        "asjcd,jdgh->asjcgh", blocks, w_gate_up, preferred_element_type=jnp.float32
    )
    unit_values = (jax.nn.silu(pre_act[..., 0, :]) * pre_act[..., 1, :]).astype(jnp.bfloat16)
    summed_here = jnp.einsum(
        "asjcf,jfd->asjcd",
        lax.all_gather(unit_values, "tp", axis=4, tiled=True),
        w_down,
        preferred_element_type=jnp.float32,
    )
    out_width = w_down.shape[2]
    reduced = lax.psum_scatter(
        summed_here.astype(jnp.bfloat16), "attn", scatter_dimension=0, tiled=True
    )
    returned = lax.all_to_all(reduced, "exp", split_axis=1, concat_axis=1, tiled=True)
    outputs = returned.reshape(slot_total, out_width)
    columns = slot_ids[None, :]
    picker = route_weights[:, 0:1] * (columns == target[:, 0:1]).astype(jnp.float32)
    picker = picker + route_weights[:, 1:2] * (columns == target[:, 1:2]).astype(jnp.float32)
    moe_out = jnp.dot(picker, outputs.astype(jnp.float32), precision=lax.Precision.HIGHEST).astype(
        jnp.bfloat16
    )
    return (attn_out, moe_out)


def solution(mesh):
    return jax.shard_map(
        body,
        mesh=mesh,
        in_specs=(
            P(("attn", "exp"), "tp"),
            P(("attn", "exp"), "tp", None, None),
            P(("attn", "exp"), "tp", None, None),
            P(("attn", "exp"), "tp"),
            P(("attn", "exp"), "tp"),
            P(("attn", "exp")),
            P(("attn", "exp"), "tp"),
            P(),
            P(("attn", "exp"), None),
            P(("attn", "exp"), None),
            P("exp", None, None, ("attn", "tp")),
            P("exp", "attn", "tp"),
        ),
        out_specs=(P(("attn", "exp"), "tp"), P(("attn", "exp"), "tp")),
        check_vma=False,
    )
```

profile of v0, /device:TPU:64, one launch (start us, length us, event | category | flops | bytes accessed | tf_op | source)
XLA Modules:
  0.0 332.8 jit_solution(8491310567244017823)
XLA Ops:
  7.2 0.9 reshape.180
  8.1 0.7 iota_compare_fusion.4
  8.9 0.7 convert_element_type.76
  9.6 0.8 fusion.38
  10.4 1.2 fusion.48
  11.6 0.2 fusion.30
  11.8 0.8 copy.37
  12.8 0.2 select_reduce_fusion
  13.2 0.7 multiply_add_fusion
  14.0 1.2 fusion.19
  15.2 1.3 add_convert_fusion
  16.5 30.1 %all_gather.6 = bf16[24,3072]{1,0:T(8,128)(2,1)S(1)} all-gather(bf16[24,384]{1,0:T(8,128)(2,1)S(1)} %get-tuple-element.2), channel_id=1, replica_groups=mesh['attn'=8,'tp'=8,'exp'=8] {'tp'}, dimensions={1}, use_global_device_ids=true | all-gather | bytes 165888 | tf_op jit(solution)/shard_map/all_gather | solution.py:71
  46.7 1.9 convolution_convert_fusion
  48.7 2.1 broadcast_in_dim.18
  50.7 1.9 broadcast_in_dim.19
  52.6 150.2 %all_to_all.10 = bf16[64,12,3072]{2,1,0:T(8,128)(2,1)S(1)} all-to-all(bf16[64,12,3072]{2,1,0:T(8,128)(2,1)S(1)} %bitcast.83), channel_id=1, replica_groups=mesh['attn'=8,'tp'=8,'exp'=8] {'attn','exp'}, dimensions={0} | all-to-all | bytes 9437184 | tf_op jit(solution)/shard_map/all_to_all | solution.py:89
  202.9 3.4 %fusion.4 = f32[8,8,1,12,2,256]{5,3,4,1,0,2:T(8,128)S(1)} fusion(bf16[8,8,12,3072,1]{3,2,4,1,0:T(8,128)(2,1)S(1)} %bitcast.84, bf16[3072,2,256,1,1]{2,1,0,4,3:T(2,128)(2,1)S(1)} %bitcast.82), kind=kOutput, calls=%fused_computation.5 | convolution fusion | flops 2415919104 | bytes 9437184 | tf_op jit(solution)/shard_map/asjcd,jdgh->asjcgh/dot_general | solution.py:94
  206.3 1.1 fusion.21
  207.5 62.9 %all-gather.2.cloned.1.call-done = bf16[8,8,1,12,2048]{4,3,1,0,2:T(8,128)(2,1)} async-done(((bf16[8,8,1,12,256]{4,3,1,0,2:T(8,128)(2,1)}), bf16[8,8,1,12,2048]{4,3,1,0,2:T(8,128)(2,1)}) %all-gather.2.cloned.1.call-update) | async-done | bytes 3145744 | tf_op jit(solution)/shard_map/all_gather | solution.py:100
  270.4 5.9 %fusion.13 = bf16[8,8,1,12,384]{4,3,1,0,2:T(8,128)(2,1)} fusion(bf16[1,2048,384]{2,1,0:T(8,128)(2,1)} %param.23, bf16[8,8,1,12,2048]{4,3,1,0,2:T(8,128)(2,1)} %all-gather.2.cloned.1.call-done), kind=kOutput, calls=%fused_computation.8 | convolution fusion | flops 1208254464 | bytes 5308416 | tf_op jit(solution)/shard_map/asjcf,jfd->asjcd/dot_general | solution.py:98
  276.3 33.3 %reduce-scatter.2.cloned.1.call-done = bf16[1,8,1,12,384]{4,3,1,0,2:T(8,128)(2,1)} async-done(((bf16[8,8,1,12,384]{4,3,1,0,2:T(8,128)(2,1)}), bf16[1,8,1,12,384]{4,3,1,0,2:T(8,128)(2,1)}) %reduce-scatter.2.cloned.1.call-update) | async-done | bytes 73744 | tf_op jit(solution)/shard_map/reduce_scatter | solution.py:105
  309.6 6.7 %all-to-all-start.1 = ((bf16[1,8,1,12,384]{4,3,0,2,1:T(8,128)(2,1)}), bf16[1,8,1,12,384]{4,3,0,2,1:T(8,128)(2,1)S(1)}, u32[]{:S(2)}, u32[]{:S(2)}) async-start(bf16[1,8,1,12,384]{4,3,0,2,1:T(8,128)(2,1)} %bitcast.85), calls=%async_computation.2 | async-start | bytes 196608 | tf_op jit(solution)/shard_map/all_to_all | solution.py:108
  316.4 8.7 %all-to-all-done.1 = bf16[1,8,1,12,384]{4,3,0,2,1:T(8,128)(2,1)S(1)} async-done(((bf16[1,8,1,12,384]{4,3,0,2,1:T(8,128)(2,1)}), bf16[1,8,1,12,384]{4,3,0,2,1:T(8,128)(2,1)S(1)}, u32[]{:S(2)}, u32[]{:S(2)}) %all-to-all-start.1) | async-done | bytes 73760 | tf_op jit(solution)/shard_map/all_to_all | solution.py:108
  325.1 0.8 convolution_convert_fusion.1
  (21 shorter events, 0.8 us)
Async XLA Ops:
  7.2 195.7 %copy-start = (bf16[1,3072,2,256]{3,2,1,0:T(2,128)(2,1)S(1)}, bf16[1,3072,2,256]{3,2,1,0:T(2,128)(2,1)}, u32[]{:S(2)}) copy-start(bf16[1,3072,2,256]{3,2,1,0:T(2,128)(2,1)} %param.22) | copy-start | bytes 9437188
  7.2 263.3 %all-gather.2.cloned.1.call-start = ((), (), s32[]{:S(2)}) async-start(), calls=%async_computation.3 | async-start | bytes 4718592 | tf_op jit(solution)/shard_map/all_gather | solution.py:100
  207.4 108.9 %copy-start.1 = (f32[24,2]{0,1:T(2,128)S(1)}, f32[24,2]{0,1:T(2,128)}, u32[]{:S(2)}) copy-start(f32[24,2]{0,1:T(2,128)} %param.21) | copy-start | bytes 580
  207.4 102.2 %reduce-scatter.2.cloned.1.call-start = ((), (), s32[]{:S(2)}) async-start(), calls=%async_computation.4 | async-start | bytes 884736 | tf_op jit(solution)/shard_map/reduce_scatter | solution.py:105
  309.6 15.5 %all-to-all-start.1 = ((bf16[1,8,1,12,384]{4,3,0,2,1:T(8,128)(2,1)}), bf16[1,8,1,12,384]{4,3,0,2,1:T(8,128)(2,1)S(1)}, u32[]{:S(2)}, u32[]{:S(2)}) async-start(bf16[1,8,1,12,384]{4,3,0,2,1:T(8,128)(2,1)} %bitcast.85), calls=%async_computation.2 | async-start | bytes 196608 | tf_op jit(solution)/shard_map/all_to_all | solution.py:108
Sparse Core Ops, SparseCore 0:
  207.6 62.8 all-gather.1
  276.5 33.1 reduce-scatter.1
where the time goes:
time: 333 us
  blocking collectives  180 us (54%)
  waiting for transfers between devices  105 us (32%)
  matrix products  15.3 us (5%)
  between operations  14.1 us (4%)
  starting transfers between devices  6.82 us (2%)
  local copies, waits for them, and re-layouts  5.94 us (2%)
  other arithmetic  5.37 us (2%)
    all_to_all x1, blocking collectives, body(): lax.all_to_all(spread, ('attn', 'exp'), split_axis=0, concat_axis=0, tile...  150 us
    all_gather x1, waiting for transfers between devices, body(): lax.all_gather(unit_values, 'tp', axis=4, tiled=True)  62.9 us
    reduce_scatter x1, waiting for transfers between devices, body(): lax.psum_scatter(summed_here.astype(jnp.bfloat16), 'attn', scatter_dimens...  33.3 us
    all_gather x1, blocking collectives, body(): hidden = lax.all_gather(hidden_part, 'tp', axis=1, tiled=True)  30.1 us
    all_to_all x1, waiting for transfers between devices, body(): lax.all_to_all(reduced, 'exp', split_axis=1, concat_axis=1, tiled=True)  8.71 us
    all_to_all x1, starting transfers between devices, body(): lax.all_to_all(reduced, 'exp', split_axis=1, concat_axis=1, tiled=True)  6.74 us
  transfers between devices with their start and end apart: 3, of which 3 were waited for; matrix products, arithmetic and copies ran while one was open for 0% of the time, Pallas kernels for 0%

commit v1 on v0

v1 whole, which is shorter than its diff:
```python
import math

import jax
import jax.numpy as jnp
from jax import lax
from jax.experimental import pallas as pl
from jax.experimental.pallas import tpu as pltpu
from jax.sharding import Mesh, PartitionSpec as P

HD = 128
EXPERTS = 8


def attend_local(queries, key_cache, value_cache, new_key, new_value, lengths):
    row_count = key_cache.shape[0]
    kv_local = key_cache.shape[1]
    query_heads = queries.reshape(row_count, kv_local, -1, HD)
    fresh_key = new_key.reshape(row_count, kv_local, HD)
    fresh_value = new_value.reshape(row_count, kv_local, HD)
    score_scale = 1.0 / math.sqrt(HD)
    scores = (
        jnp.einsum("rkgd,rkpd->rkgp", query_heads, key_cache, preferred_element_type=jnp.float32)
        * score_scale
    )
    own_score = (
        jnp.einsum("rkgd,rkd->rkg", query_heads, fresh_key, preferred_element_type=jnp.float32)
        * score_scale
    )
    valid = (
        jnp.arange(key_cache.shape[2], dtype=jnp.int32)[None, None, None, :]
        < lengths[:, None, None, None]
    )
    masked = jnp.where(valid, scores, -jnp.inf)
    row_max = jnp.maximum(jnp.max(masked, axis=-1), own_score)
    exp_terms = jnp.exp(masked - row_max[..., None])
    own_term = jnp.exp(own_score - row_max)
    denominator = jnp.sum(exp_terms, axis=-1) + own_term
    probs = (exp_terms / denominator[..., None]).astype(jnp.bfloat16)
    probs_new = (own_term / denominator).astype(jnp.bfloat16)
    attended = jnp.einsum("rkgp,rkpd->rkgd", probs, value_cache, preferred_element_type=jnp.float32)
    attended = (
        attended
        + probs_new.astype(jnp.float32)[..., None] * fresh_value.astype(jnp.float32)[:, :, None, :]
    )
    return attended.reshape(row_count, -1).astype(jnp.bfloat16)


def slots_of(block_routes):
    flat_routes = block_routes.reshape(-1)
    onehot = (flat_routes[:, None] == jnp.arange(EXPERTS, dtype=jnp.int32)[None, :]).astype(
        jnp.int32
    )
    before = jnp.cumsum(onehot, axis=0) - onehot
    return jnp.sum(before * onehot, axis=1).reshape(block_routes.shape)


def shift(value, axis, step):
    size = lax.axis_size(axis)
    return lax.ppermute(value, axis, [(i, (i + step) % size) for i in range(size)])


def down_kernel(units_ref, own_ref, other_ref, out_ref, total_ref):
    step = pl.program_id(0)
    half = own_ref.shape[0]

    @pl.when(step == 0)
    def _():
        total_ref[...] = jnp.zeros_like(total_ref)

    total_ref[...] += jnp.dot(
        units_ref[0, :, :half], own_ref[...], preferred_element_type=jnp.float32
    ) + jnp.dot(units_ref[0, :, half:], other_ref[...], preferred_element_type=jnp.float32)

    @pl.when(step == pl.num_programs(0) - 1)
    def _():
        out_ref[...] = total_ref[...].astype(out_ref.dtype)


def down_project(units, own, other):
    groups, rows, width = units.shape
    half, cols = width // 2, own.shape[1]
    return pl.pallas_call(
        down_kernel,
        grid=(groups,),
        in_specs=[
            pl.BlockSpec((1, rows, width), lambda z: (z, 0, 0)),
            pl.BlockSpec((half, cols), lambda z: (z, 0)),
            pl.BlockSpec((half, cols), lambda z: (z, 0)),
        ],
        out_specs=pl.BlockSpec((rows, cols), lambda z: (0, 0)),
        out_shape=jax.ShapeDtypeStruct((rows, cols), jnp.bfloat16),
        scratch_shapes=[pltpu.VMEM((rows, cols), jnp.float32)],
        compiler_params=pltpu.CompilerParams(vmem_limit_bytes=24 * 1024 * 1024),
        cost_estimate=pl.CostEstimate(
            flops=2 * groups * rows * width * cols,
            bytes_accessed=2 * (groups * rows * width + 2 * own.size + rows * cols),
            transcendentals=0,
        ),
    )(units, own, other)


def body(
    queries,
    key_cache,
    value_cache,
    new_key,
    new_value,
    lengths,
    residual,
    norm_gain,
    routes,
    route_weights,
    w_gate_up,
    w_down,
):
    gate_up_own, down_own = w_gate_up[0], w_down[0]
    gate_up_other, down_other = shift(gate_up_own, "core", 1), shift(down_own, "core", 1)

    attn_out = attend_local(queries, key_cache, value_cache, new_key, new_value, lengths)
    hidden_part = (residual.astype(jnp.float32) + attn_out.astype(jnp.float32)).astype(jnp.bfloat16)
    n_x, n_tp, n_exp = lax.axis_size("x"), lax.axis_size("tp"), lax.axis_size("exp")
    row_count, part = hidden_part.shape
    copies = jnp.broadcast_to(hidden_part[None], (n_tp, row_count, part))
    hidden = lax.all_to_all(copies, "tp", split_axis=0, concat_axis=0, tiled=True)
    hidden_wide = hidden.astype(jnp.float32)
    feature_count = n_tp * part
    mean_square = jnp.sum(hidden_wide * hidden_wide, axis=(0, 2)) / feature_count
    inv_rms = lax.rsqrt(mean_square + 1e-05)
    gain = norm_gain.reshape(n_tp, 1, part)
    normed = (hidden_wide * inv_rms[None, :, None] * gain).astype(jnp.bfloat16)

    capacity = row_count // 2
    slot_total = EXPERTS * capacity
    target = routes * capacity + slots_of(routes)
    slot_ids = jnp.arange(slot_total, dtype=jnp.int32)
    placement = jnp.any(slot_ids[:, None, None] == target[None, :, :], axis=2).astype(jnp.bfloat16)
    normed = jnp.swapaxes(normed, 0, 1).reshape(row_count, feature_count)
    packed = jnp.dot(placement, normed, preferred_element_type=jnp.float32).astype(jnp.bfloat16)
    packed = packed.reshape(n_exp, capacity, feature_count)
    arrived = lax.all_to_all(packed, "exp", split_axis=0, concat_axis=0, tiled=True)
    own_rows = arrived.reshape(n_exp * capacity, feature_count)

    blocks = [own_rows] + [shift(own_rows, "x", k) for k in range(1, n_x)]
    rows = jnp.concatenate(blocks, axis=0)

    def units_of(weights):
        pre_act = jnp.einsum("rd,dgh->rgh", rows, weights, preferred_element_type=jnp.float32)
        return (jax.nn.silu(pre_act[:, 0]) * pre_act[:, 1]).astype(jnp.bfloat16)

    units = jnp.concatenate([units_of(gate_up_own), units_of(gate_up_other)], axis=1)
    gathered = lax.all_gather(units, "tp", axis=0, tiled=True)
    gathered = gathered.reshape(n_tp, units.shape[0], units.shape[1])
    partial = down_project(gathered, down_own, down_other)

    partial = partial.reshape(n_x, n_exp, capacity, part)
    x_index = lax.axis_index("x")
    order = (x_index - jnp.arange(n_x, dtype=jnp.int32)) % n_x
    partial = jnp.take(partial, order, axis=0)
    partial = partial.reshape(n_x * n_exp, capacity, part)
    returned = lax.all_to_all(partial, ("x", "exp"), split_axis=0, concat_axis=0, tiled=True)
    outputs = returned.reshape(n_x * slot_total, part)
    columns = slot_ids[None, :]
    picker = route_weights[:, 0:1] * (columns == target[:, 0:1]).astype(jnp.float32)
    picker = picker + route_weights[:, 1:2] * (columns == target[:, 1:2]).astype(jnp.float32)
    picker = jnp.tile(picker, (1, n_x))
    moe_out = jnp.dot(picker, outputs.astype(jnp.float32), precision=lax.Precision.HIGHEST).astype(
        jnp.bfloat16
    )
    return (attn_out, moe_out)


def solution(mesh):
    sizes = mesh.shape
    cores = 2
    chips = Mesh(
        mesh.devices.reshape(sizes["attn"] // cores, cores, sizes["tp"], sizes["exp"]),
        ("x", "core", "tp", "exp"),
    )
    rows = ("x", "core", "exp")
    return jax.shard_map(
        body,
        mesh=chips,
        in_specs=(
            P(rows, "tp"),
            P(rows, "tp", None, None),
            P(rows, "tp", None, None),
            P(rows, "tp"),
            P(rows, "tp"),
            P(rows),
            P(rows, "tp"),
            P(),
            P(rows, None),
            P(rows, None),
            P("exp", None, None, ("x", "core", "tp")),
            P("exp", ("x", "core"), "tp"),
        ),
        out_specs=(P(rows, "tp"), P(rows, "tp")),
        check_vma=False,
    )
```

time: 333 us -> 203 us (0.61)
  the two profiles are of different devices: /device:TPU:64 before, /device:TPU:8 now
where the time goes in v1:
time: 203 us; the launch traced here: 202 us
  waiting for transfers between devices  79.8 us (39%)
  starting transfers between devices  35.5 us (17%)
  blocking collectives  30 us (15%)
  local copies, waits for them, and re-layouts  18.9 us (9%)
  between operations  14.3 us (7%)
  matrix products  10.9 us (5%)
  other arithmetic  6.37 us (3%)
  Pallas kernels  6.21 us (3%)
    all_gather x1, waiting for transfers between devices, body(): gathered = lax.all_gather(units, 'tp', axis=0, tiled=True)  45.2 us
    all_to_all x1, blocking collectives, body(): lax.all_to_all(packed, 'exp', split_axis=0, concat_axis=0, tiled=True)  30 us
    ppermute x5, waiting for transfers between devices, shift(): lax.ppermute(value, axis, [(i, (i + step) % size) for i in range(size)])  21.1 us
    ppermute x5, starting transfers between devices, shift(): lax.ppermute(value, axis, [(i, (i + step) % size) for i in range(size)])  15.3 us
    all_to_all x1, waiting for transfers between devices, body(): lax.all_to_all(partial, ('x', 'exp'), split_axis=0, concat_axis=0, tiled=...  13.5 us
    all_to_all x1, starting transfers between devices, body(): lax.all_to_all(copies, 'tp', split_axis=0, concat_axis=0, tiled=True)  10.3 us
    all_to_all x1, starting transfers between devices, body(): lax.all_to_all(partial, ('x', 'exp'), split_axis=0, concat_axis=0, tiled=...  9.84 us
    unnamed x14, local copies, waits for them, and re-layouts  7.83 us
  transfers between devices with their start and end apart: 8, of which 5 were waited for; matrix products, arithmetic and copies ran while one was open for 10% of the time, Pallas kernels for 0%

profile of v1, /device:TPU:8, one launch (start us, length us, event | category | flops | bytes accessed | tf_op | source)
XLA Modules:
  0.0 202.0 jit_solution(16395282751879818223)
XLA Ops:
  9.5 1.2 fusion.29
  11.9 1.3 add_convert_fusion
  13.9 10.3 %all-to-all-start = ((bf16[8,24,384]{2,1,0:T(8,128)(2,1)}), bf16[8,24,384]{2,1,0:T(8,128)(2,1)S(1)}, u32[]{:S(2)}, u32[]{:S(2)}) async-start(bf16[8,24,384]{2,1,0:T(8,128)(2,1)} %broadcast_in_dim.48), calls=%async_computation | async-start | bytes 294912 | tf_op jit(solution)/shard_map/all_to_all | solution.py:124
  24.3 7.0 %copy.40 = bf16[1,3072,2,256]{1,3,2,0:T(8,128)(2,1)S(1)} copy(bf16[1,3072,2,256]{3,2,1,0:T(2,128)(2,1)} %param.22) | data formatting | bytes 6291456 | tf_op args[10]
  31.3 1.9 collective-permute-start.3
  35.1 1.2 convolution_convert_fusion
  36.2 2.1 %reshape.252 = bf16[8,12,3072]{2,1,0:T(8,128)(2,1)} reshape(bf16[96,3072]{1,0:T(8,128)(2,1)} %convolution_convert_fusion) | data formatting | bytes 1179648 | tf_op jit(solution)/shard_map/reshape | solution.py:139
  38.3 30.0 %all_to_all.15 = bf16[8,12,3072]{2,1,0:T(8,128)(2,1)} all-to-all(bf16[8,12,3072]{2,1,0:T(8,128)(2,1)} %reshape.252), channel_id=1, replica_groups=mesh['x'=4,'core'=2,'tp'=8,'exp'=8] {'exp'}, dimensions={0} | all-to-all | bytes 1179648 | tf_op jit(solution)/shard_map/all_to_all | solution.py:140
  68.2 2.1 %reshape.253 = bf16[96,3072]{1,0:T(8,128)(2,1)} reshape(bf16[8,12,3072]{2,1,0:T(8,128)(2,1)} %all_to_all.15) | data formatting | bytes 1179648 | tf_op jit(solution)/shard_map/reshape | solution.py:141
  70.3 3.5 %collective-permute-start = (bf16[96,3072]{1,0:T(8,128)(2,1)}, bf16[96,3072]{1,0:T(8,128)(2,1)S(1)}, u32[]{:S(2)}, u32[]{:S(2)}) collective-permute-start(bf16[96,3072]{1,0:T(8,128)(2,1)} %reshape.253), channel_id=1, source_target_pairs={{0,128},{128,256},{256,384},{384,0},{1,129},{129,257},{257,385},{3... | collective-permute-start | bytes 1769480 | tf_op jit(solution)/shard_map/ppermute | solution.py:59
  73.9 4.6 %collective-permute-start.1 = (bf16[96,3072]{1,0:T(8,128)(2,1)}, bf16[96,3072]{1,0:T(8,128)(2,1)S(1)}, u32[]{:S(2)}, u32[]{:S(2)}) collective-permute-start(bf16[96,3072]{1,0:T(8,128)(2,1)} %reshape.253), channel_id=1, source_target_pairs={{0,256},{128,384},{256,0},{384,128},{1,257},{129,385},{257,1},{385... | collective-permute-start | bytes 1769480 | tf_op jit(solution)/shard_map/ppermute | solution.py:59
  78.5 3.3 %collective-permute-start.2 = (bf16[96,3072]{1,0:T(8,128)(2,1)}, bf16[96,3072]{1,0:T(8,128)(2,1)S(1)}, u32[]{:S(2)}, u32[]{:S(2)}) collective-permute-start(bf16[96,3072]{1,0:T(8,128)(2,1)} %reshape.253), channel_id=1, source_target_pairs={{0,384},{128,0},{256,128},{384,256},{1,385},{129,1},{257,129},{385... | collective-permute-start | bytes 1769480 | tf_op jit(solution)/shard_map/ppermute | solution.py:59
  81.9 7.2 %collective-permute-done = bf16[96,3072]{1,0:T(8,128)(2,1)S(1)} collective-permute-done((bf16[96,3072]{1,0:T(8,128)(2,1)}, bf16[96,3072]{1,0:T(8,128)(2,1)S(1)}, u32[]{:S(2)}, u32[]{:S(2)}) %collective-permute-start) | collective-permute-done | bytes 589856 | tf_op jit(solution)/shard_map/ppermute | solution.py:59
  89.0 12.3 %collective-permute-done.1 = bf16[96,3072]{1,0:T(8,128)(2,1)S(1)} collective-permute-done((bf16[96,3072]{1,0:T(8,128)(2,1)}, bf16[96,3072]{1,0:T(8,128)(2,1)S(1)}, u32[]{:S(2)}, u32[]{:S(2)}) %collective-permute-start.1) | collective-permute-done | bytes 589856 | tf_op jit(solution)/shard_map/ppermute | solution.py:59
  101.4 1.5 collective-permute-done.2
  102.9 2.9 %fusion.3 = f32[384,2,256]{0,2,1:T(8,128)S(1)} fusion(bf16[96,3072]{1,0:T(8,128)(2,1)S(1)} %collective-permute-done.2, bf16[96,3072]{1,0:T(8,128)(2,1)S(1)} %collective-permute-done.1, bf16[96,3072]{1,0:T(8,128)(2,1)S(1)} %collective-permute-done, bf16[96,3072]{1,0:T(8,128)(2,1)} %reshape.253, bf16[1,3072,2,256]{1,3,2,0:T(8,128)(2,1)S(1)} %copy.40), kind=kOutput, calls=%fused_computation.9 | convolution fusion | flops 1217396736 | bytes 6291456 | tf_op jit(solution)/shard_map/rd,dgh->rgh/dot_general | solution.py:147
  105.9 3.7 %fusion.2 = f32[384,2,256]{0,2,1:T(8,128)S(1)} fusion(bf16[3072,2,256]{0,2,1:T(8,128)(2,1)} %collective-permute-done.3, bf16[96,3072]{1,0:T(8,128)(2,1)S(1)} %collective-permute-done.2, bf16[96,3072]{1,0:T(8,128)(2,1)S(1)} %collective-permute-done.1, bf16[96,3072]{1,0:T(8,128)(2,1)S(1)} %collective-permute-done, bf16[96,3072]{1,0:T(8,128)(2,1)S(1)} %copy-done.2), kind=kOutput, calls=%fused_computation.8 | convolution fusion | flops 1217396736 | bytes 6291456 | tf_op jit(solution)/shard_map/rd,dgh->rgh/dot_general | solution.py:147
  110.6 1.9 collective-permute-start.4
  112.8 45.2 %all-gather.2.cloned.1.call-done = bf16[3072,512]{0,1:T(8,128)(2,1)} async-done(((bf16[384,512]{0,1:T(8,128)(2,1)}), bf16[3072,512]{0,1:T(8,128)(2,1)}) %all-gather.2.cloned.1.call-update) | async-done | bytes 3145744 | tf_op jit(solution)/shard_map/all_gather | solution.py:151
  158.0 3.2 %copy.41 = bf16[3072,512]{1,0:T(8,128)(2,1)S(1)} copy(bf16[3072,512]{0,1:T(8,128)(2,1)} %all-gather.2.cloned.1.call-done) | data formatting | bytes 6291456 | tf_op jit(solution)/shard_map/all_gather | solution.py:151
  161.2 6.2 %shard_map.131 = bf16[384,384]{1,0:T(8,128)(2,1)S(1)} custom-call(bf16[8,384,512]{2,1,0:T(8,128)(2,1)S(1)} %bitcast.67, bf16[2048,384]{1,0:T(8,128)(2,1)} %bitcast.17.own_ref, bf16[2048,384]{1,0:T(8,128)(2,1)} %collective-permute-done.4.other_ref), custom_call_target="tpu_custom_call" | custom-call | flops 1207959552 | bytes 6586368 | tf_op jit(solution)/shard_map/pallas_call | solution.py:82
  168.1 1.0 reshape.255
  170.6 9.8 %all-to-all-start.2 = ((bf16[32,12,384]{2,1,0:T(8,128)(2,1)}), bf16[32,12,384]{2,1,0:T(8,128)(2,1)S(1)}, u32[]{:S(2)}, u32[]{:S(2)}) async-start(bf16[32,12,384]{2,1,0:T(8,128)(2,1)} %bitcast_select_fusion), calls=%async_computation.2 | async-start | bytes 786432 | tf_op jit(solution)/shard_map/all_to_all | solution.py:160
  180.7 13.5 %all-to-all-done.2 = bf16[32,12,384]{2,1,0:T(8,128)(2,1)S(1)} async-done(((bf16[32,12,384]{2,1,0:T(8,128)(2,1)}), bf16[32,12,384]{2,1,0:T(8,128)(2,1)S(1)}, u32[]{:S(2)}, u32[]{:S(2)}) %all-to-all-start.2) | async-done | bytes 294944 | tf_op jit(solution)/shard_map/all_to_all | solution.py:160
  (57 shorter events, 10.6 us)
Async XLA Ops:
  7.2 4.5 %copy-start = (bf16[24,1,32,128]{3,2,1,0:T(8,128)(2,1)S(1)}, bf16[24,1,32,128]{3,2,1,0:T(8,128)(2,1)}, u32[]{:S(2)}) copy-start(bf16[24,1,32,128]{3,2,1,0:T(8,128)(2,1)} %param.14) | copy-start | bytes 589828
  13.9 20.8 %all-to-all-start = ((bf16[8,24,384]{2,1,0:T(8,128)(2,1)}), bf16[8,24,384]{2,1,0:T(8,128)(2,1)S(1)}, u32[]{:S(2)}, u32[]{:S(2)}) async-start(bf16[8,24,384]{2,1,0:T(8,128)(2,1)} %broadcast_in_dim.48), calls=%async_computation | async-start | bytes 294912 | tf_op jit(solution)/shard_map/all_to_all | solution.py:124
  24.2 9.0 %copy-start.3 = (f32[3072]{0:T(1024)S(1)}, f32[3072]{0:T(1024)}, u32[]{:S(2)}) copy-start(f32[3072]{0:T(1024)} %param.19) | copy-start | bytes 36868
  24.2 9.0 %copy-start.4 = (s32[24,2]{0,1:T(2,128)S(1)}, s32[24,2]{0,1:T(2,128)}, u32[]{:S(2)}) copy-start(s32[24,2]{0,1:T(2,128)} %param.20) | copy-start | bytes 580
  24.2 133.7 %all-gather.2.cloned.1.call-start = ((), (), s32[]{:S(2)}) async-start(), calls=%async_computation.3 | async-start | bytes 3538944 | tf_op jit(solution)/shard_map/all_gather | solution.py:151
  31.3 74.6 %collective-permute-start.3 = (bf16[3072,2,256]{0,2,1:T(8,128)(2,1)S(1)}, bf16[3072,2,256]{0,2,1:T(8,128)(2,1)}, u32[]{:S(2)}, u32[]{:S(2)}) collective-permute-start(bf16[3072,2,256]{0,2,1:T(8,128)(2,1)S(1)} %bitcast.68), channel_id=1, source_target_pairs={{0,64},{64,0},{1,65},{65,1},{2,66},{66,2},{3,67},{67,3},{4,68},{68... | collective-permute-start | bytes 9437192 | tf_op jit(solution)/shard_map/ppermute | solution.py:59
  70.3 35.6 %copy-start.2 = (bf16[96,3072]{1,0:T(8,128)(2,1)S(1)}, bf16[96,3072]{1,0:T(8,128)(2,1)}, u32[]{:S(2)}) copy-start(bf16[96,3072]{1,0:T(8,128)(2,1)} %reshape.253) | copy-start | bytes 1769476
  70.3 18.7 %collective-permute-start = (bf16[96,3072]{1,0:T(8,128)(2,1)}, bf16[96,3072]{1,0:T(8,128)(2,1)S(1)}, u32[]{:S(2)}, u32[]{:S(2)}) collective-permute-start(bf16[96,3072]{1,0:T(8,128)(2,1)} %reshape.253), channel_id=1, source_target_pairs={{0,128},{128,256},{256,384},{384,0},{1,129},{129,257},{257,385},{3... | collective-permute-start | bytes 1769480 | tf_op jit(solution)/shard_map/ppermute | solution.py:59
  73.9 27.5 %collective-permute-start.1 = (bf16[96,3072]{1,0:T(8,128)(2,1)}, bf16[96,3072]{1,0:T(8,128)(2,1)S(1)}, u32[]{:S(2)}, u32[]{:S(2)}) collective-permute-start(bf16[96,3072]{1,0:T(8,128)(2,1)} %reshape.253), channel_id=1, source_target_pairs={{0,256},{128,384},{256,0},{384,128},{1,257},{129,385},{257,1},{385... | collective-permute-start | bytes 1769480 | tf_op jit(solution)/shard_map/ppermute | solution.py:59
  78.5 24.4 %collective-permute-start.2 = (bf16[96,3072]{1,0:T(8,128)(2,1)}, bf16[96,3072]{1,0:T(8,128)(2,1)S(1)}, u32[]{:S(2)}, u32[]{:S(2)}) collective-permute-start(bf16[96,3072]{1,0:T(8,128)(2,1)} %reshape.253), channel_id=1, source_target_pairs={{0,384},{128,0},{256,128},{384,256},{1,385},{129,1},{257,129},{385... | collective-permute-start | bytes 1769480 | tf_op jit(solution)/shard_map/ppermute | solution.py:59
  110.6 50.6 %collective-permute-start.4 = (bf16[2048,384]{1,0:T(8,128)(2,1)}, bf16[2048,384]{1,0:T(8,128)(2,1)}, u32[]{:S(2)}, u32[]{:S(2)}) collective-permute-start(bf16[2048,384]{1,0:T(8,128)(2,1)} %bitcast.17.own_ref), channel_id=1, source_target_pairs={{0,64},{64,0},{1,65},{65,1},{2,66},{66,2},{3,67},{67,3},{4,68},{68... | collective-permute-start | bytes 4718600 | tf_op jit(solution)/shard_map/ppermute | solution.py:59
  161.2 19.3 %copy-start.5 = (f32[24,2]{0,1:T(2,128)S(1)}, f32[24,2]{0,1:T(2,128)}, u32[]{:S(2)}) copy-start(f32[24,2]{0,1:T(2,128)} %param.21) | copy-start | bytes 580
  167.4 0.7 copy-start.1
  170.6 23.5 %all-to-all-start.2 = ((bf16[32,12,384]{2,1,0:T(8,128)(2,1)}), bf16[32,12,384]{2,1,0:T(8,128)(2,1)S(1)}, u32[]{:S(2)}, u32[]{:S(2)}) async-start(bf16[32,12,384]{2,1,0:T(8,128)(2,1)} %bitcast_select_fusion), calls=%async_computation.2 | async-start | bytes 786432 | tf_op jit(solution)/shard_map/all_to_all | solution.py:160
Sparse Core Ops, SparseCore 0:
  110.7 47.1 all-gather.1

commit v2 on v1

v2 whole, which is shorter than its diff:
```python
import functools
import math

import jax
import jax.numpy as jnp
from jax import lax
from jax.experimental import pallas as pl
from jax.experimental.pallas import tpu as pltpu
from jax.sharding import Mesh, PartitionSpec as P

HD = 128
EXPERTS = 8


def front_kernel(*refs):
    sources, (attn_ref, packed_ref, picker_ref), scratch = refs[:9], refs[9:12], refs[12:]
    landed, (query_rows, key_rows, value_rows, attended_rows, packed_rows, sems) = (
        scratch[:9],
        scratch[9:],
    )
    copies = [
        pltpu.make_async_copy(source, place, sems.at[index])
        for index, (source, place) in enumerate(zip(sources, landed))
    ]
    for copy in copies:
        copy.start()

    lengths_ref, routes_ref, route_weights_ref = landed[:3]
    for copy in copies[:3]:
        copy.wait()
    copy_count, experts, capacity, _ = packed_ref.shape
    row_count = routes_ref.shape[1]
    routes = routes_ref[...]
    expert_ids = lax.broadcasted_iota(jnp.int32, (experts, row_count), 0)
    first = (routes[0:1] == expert_ids).astype(jnp.float32)
    second = (routes[1:2] == expert_ids).astype(jnp.float32)
    row_ids = lax.broadcasted_iota(jnp.int32, (row_count, row_count), 0)
    later = row_ids < lax.broadcasted_iota(jnp.int32, (row_count, row_count), 1)
    before = jnp.dot(first + second, later.astype(jnp.float32), preferred_element_type=jnp.float32)
    slots = [
        jnp.sum(before * first, axis=0, keepdims=True),
        jnp.sum((before + first) * second, axis=0, keepdims=True),
    ]
    slot_total = experts * capacity
    slot_ids = lax.broadcasted_iota(jnp.int32, (slot_total, row_count), 0)
    placement = jnp.zeros(slot_ids.shape, jnp.float32)
    picker = jnp.zeros(slot_ids.shape, jnp.float32)
    for k in range(2):
        target = routes[k : k + 1] * capacity + slots[k].astype(jnp.int32)
        chosen = (slot_ids == target).astype(jnp.float32)
        placement = placement + chosen
        picker = picker + route_weights_ref[k : k + 1] * chosen
    for copy in range(copy_count):
        picker_ref[copy * slot_total : (copy + 1) * slot_total] = picker

    for copy in copies[3:]:
        copy.wait()
    queries_ref, new_key_ref, new_value_ref, residual_ref, keys_ref, values_ref = landed[3:]
    cached = keys_ref.shape[2]
    heads = queries_ref.shape[1] // HD
    query_rows[...] = queries_ref[...].astype(jnp.float32)
    key_rows[...] = new_key_ref[...].astype(jnp.float32)
    value_rows[...] = new_value_ref[...].astype(jnp.float32)
    score_scale = 1.0 / math.sqrt(HD)
    position = lax.broadcasted_iota(jnp.int32, (cached, 1), 0)
    for row in range(row_count):
        keys = keys_ref[row, 0].astype(jnp.float32)
        values = values_ref[row, 0].astype(jnp.float32)
        fresh_key, fresh_value = key_rows[row : row + 1], value_rows[row : row + 1]
        valid = position < lengths_ref[row]
        for head in range(heads):
            place = slice(head * HD, (head + 1) * HD)
            query = query_rows[row : row + 1, place]
            scores = jnp.sum(query * keys, axis=1, keepdims=True) * score_scale
            own_score = jnp.sum(query * fresh_key, axis=1, keepdims=True) * score_scale
            masked = jnp.where(valid, scores, -jnp.inf)
            row_max = jnp.maximum(jnp.max(masked, axis=0, keepdims=True), own_score)
            exp_terms = jnp.exp(masked - row_max)
            own_term = jnp.exp(own_score - row_max)
            denominator = jnp.sum(exp_terms, axis=0, keepdims=True) + own_term
            probs = (exp_terms / denominator).astype(jnp.bfloat16).astype(jnp.float32)
            probs_new = (own_term / denominator).astype(jnp.bfloat16).astype(jnp.float32)
            attended = jnp.sum(probs * values, axis=0, keepdims=True) + probs_new * fresh_value
            attended_rows[row : row + 1, place] = attended
    attn_out = attended_rows[...].astype(jnp.bfloat16)
    attn_ref[...] = attn_out
    hidden = residual_ref[...].astype(jnp.float32) + attn_out.astype(jnp.float32)
    packed_rows[...] = jnp.dot(
        placement.astype(jnp.bfloat16),
        hidden.astype(jnp.bfloat16),
        preferred_element_type=jnp.float32,
    )
    for expert in range(experts):
        rows = packed_rows[pl.ds(expert * capacity, capacity)].astype(jnp.bfloat16)
        for copy in range(copy_count):
            packed_ref[copy, expert] = rows


def attend_and_pack(lengths, routes, route_weights, tensors, copy_count):
    row_count, part = tensors[0].shape
    capacity = row_count // 2
    slot_total = EXPERTS * capacity
    tensors = [lengths, routes, route_weights] + tensors
    tensors = [pltpu.with_memory_space_constraint(value, pltpu.HBM) for value in tensors]
    rows = pltpu.VMEM((row_count, part), jnp.float32)
    narrow = pltpu.VMEM((row_count, HD), jnp.float32)
    vmem = pl.BlockSpec(memory_space=pltpu.VMEM)
    return pl.pallas_call(
        front_kernel,
        in_specs=[pl.BlockSpec(memory_space=pltpu.HBM)] * len(tensors),
        out_specs=[vmem] * 3,
        out_shape=[
            jax.ShapeDtypeStruct((row_count, part), jnp.bfloat16),
            jax.ShapeDtypeStruct((copy_count, EXPERTS, capacity, part), jnp.bfloat16),
            jax.ShapeDtypeStruct((copy_count * slot_total, row_count), jnp.float32),
        ],
        scratch_shapes=[pltpu.SMEM(lengths.shape, lengths.dtype)]
        + [pltpu.VMEM(value.shape, value.dtype) for value in tensors[1:]]
        + [
            rows,
            narrow,
            narrow,
            rows,
            pltpu.VMEM((slot_total, part), jnp.float32),
            pltpu.SemaphoreType.DMA((len(tensors),)),
        ],
        compiler_params=pltpu.CompilerParams(vmem_limit_bytes=24 * 1024 * 1024),
    )(*tensors)


def shift(value, axis, step):
    size = lax.axis_size(axis)
    return lax.ppermute(value, axis, [(i, (i + step) % size) for i in range(size)])


def fetch(sources, places, scratch, sems):
    width = scratch[0].shape[-2]
    copies = []
    for index, target in enumerate(scratch):
        part = pl.ds(pl.multiple_of(places[index] * width, width), width)
        group = []
        for source, ref in enumerate(sources):
            rows = ref.at[:, part] if len(ref.shape) == 3 else ref.at[part]
            group.append(pltpu.make_async_copy(rows, target.at[source], sems.at[index, source]))
            group[-1].start()
        copies.append(group)
    return copies


def up_products(place, gain_ref, row_ref, weights, total, squares):
    depth = row_ref.shape[1]
    part = pl.ds(pl.multiple_of(place * depth, depth), depth)
    rows = row_ref[...].astype(jnp.float32)
    square = rows * rows
    square = sum(square[:, lane : lane + HD] for lane in range(0, depth, HD))
    scaled = (rows * gain_ref[:, part]).astype(jnp.bfloat16)
    products = [
        jnp.dot(scaled, weights[index // 2, index % 2], preferred_element_type=jnp.float32)
        for index in range(4)
    ]
    if total is None:
        return products, square
    return [old + new for old, new in zip(total, products)], squares + square


def up_first_kernel(count, place_ref, gain_ref, own_ref, other_ref, *refs):
    row_refs, (total_ref, squares_ref, ahead_ref, weights, sems) = refs[:count], refs[-5:]
    scratch = [weights.at[index] for index in range(count)] + [ahead_ref]
    copies = fetch((own_ref, other_ref), place_ref, scratch, sems)
    total = squares = None
    for index, row_ref in enumerate(row_refs):
        for copy in copies[index]:
            copy.wait()
        total, squares = up_products(
            place_ref[index], gain_ref, row_ref, weights.at[index], total, squares
        )
    for index in range(4):
        total_ref[index] = total[index]
    squares_ref[...] = squares
    for copy in copies[count]:
        copy.wait()


def up_last_kernel(place_ref, gain_ref, row_ref, so_far_ref, squares_ref, weights_ref, out_ref):
    width = weights_ref.shape[3]
    features = gain_ref.shape[1]
    place = place_ref[place_ref.shape[0] - 1]
    so_far = [so_far_ref[index] for index in range(4)]
    total, squares = up_products(
        place, gain_ref, row_ref, weights_ref, so_far, squares_ref[...]
    )
    inv_rms = lax.rsqrt(jnp.sum(squares, axis=1, keepdims=True) / features + 1e-05)
    for index in range(2):
        gate, up = total[2 * index] * inv_rms, total[2 * index + 1] * inv_rms
        units = gate / (1.0 + jnp.exp(-gate)) * up
        out_ref[:, index * width : (index + 1) * width] = units.astype(out_ref.dtype)


def down_products(unit_ref, weights, total):
    half = unit_ref.shape[1] // 2
    for source in range(2):
        units = unit_ref[:, source * half : (source + 1) * half]
        product = jnp.dot(units, weights[source], preferred_element_type=jnp.float32)
        total = product if total is None else total + product
    return total


def down_first_kernel(count, place_ref, own_ref, other_ref, *refs):
    unit_refs, (total_ref, ahead_ref, weights, sems) = refs[:count], refs[-4:]
    scratch = [weights.at[index] for index in range(count)] + [ahead_ref]
    copies = fetch((own_ref, other_ref), place_ref, scratch, sems)
    total = None
    for index, unit_ref in enumerate(unit_refs):
        for copy in copies[index]:
            copy.wait()
        total = down_products(unit_ref, weights.at[index], total)
    total_ref[...] = total
    for copy in copies[count]:
        copy.wait()


def down_last_kernel(unit_ref, so_far_ref, weights_ref, out_ref, total_ref):
    total_ref[...] = down_products(unit_ref, weights_ref, so_far_ref[...])
    capacity = out_ref.shape[1]
    for block in range(out_ref.shape[0]):
        rows = pl.ds(block * capacity, capacity)
        out_ref[block] = total_ref[rows].astype(out_ref.dtype)


VMEM, HBM, SMEM = (
    pl.BlockSpec(memory_space=space) for space in (pltpu.VMEM, pltpu.HBM, pltpu.SMEM)
)
PARAMS = pltpu.CompilerParams(vmem_limit_bytes=24 * 1024 * 1024)


def cost(flops, bytes_accessed, transcendentals=0):
    return pl.CostEstimate(
        flops=flops, bytes_accessed=bytes_accessed, transcendentals=transcendentals
    )


def expert_units(blocks, places, gain, own, other):
    (rows, depth), width = blocks[0].shape, own.shape[2]
    own = pltpu.with_memory_space_constraint(own, pltpu.HBM)
    other = pltpu.with_memory_space_constraint(other, pltpu.HBM)
    *early, late = blocks
    count = len(early)
    weights = (2, 2, depth, width)
    sums = pl.pallas_call(
        functools.partial(up_first_kernel, count),
        in_specs=[SMEM, VMEM, HBM, HBM] + [VMEM] * count,
        out_specs=[VMEM] * 3,
        out_shape=[
            jax.ShapeDtypeStruct((4, rows, width), jnp.float32),
            jax.ShapeDtypeStruct((rows, HD), jnp.float32),
            jax.ShapeDtypeStruct(weights, jnp.bfloat16),
        ],
        scratch_shapes=[
            pltpu.VMEM((count,) + weights, jnp.bfloat16),
            pltpu.SemaphoreType.DMA((count + 1, 2)),
        ],
        compiler_params=PARAMS,
        cost_estimate=cost(8 * count * rows * depth * width, 8 * count * depth * width),
    )(places, gain, own, other, *early)
    return pl.pallas_call(
        up_last_kernel,
        in_specs=[SMEM] + [VMEM] * 5,
        out_specs=VMEM,
        out_shape=jax.ShapeDtypeStruct((rows, 2 * width), jnp.bfloat16),
        compiler_params=PARAMS,
        cost_estimate=cost(8 * rows * depth * width, 8 * depth * width, 2 * rows * width),
    )(places, gain, late, *sums)


def expert_outputs(blocks, places, own, other, shape):
    (rows, width), cols = blocks[0].shape, own.shape[1]
    own = pltpu.with_memory_space_constraint(own, pltpu.HBM)
    other = pltpu.with_memory_space_constraint(other, pltpu.HBM)
    *early, late = blocks
    count = len(early)
    weights = (2, width // 2, cols)
    sums = pl.pallas_call(
        functools.partial(down_first_kernel, count),
        in_specs=[SMEM, HBM, HBM] + [VMEM] * count,
        out_specs=[VMEM] * 2,
        out_shape=[
            jax.ShapeDtypeStruct((rows, cols), jnp.float32),
            jax.ShapeDtypeStruct(weights, jnp.bfloat16),
        ],
        scratch_shapes=[
            pltpu.VMEM((count,) + weights, jnp.bfloat16),
            pltpu.SemaphoreType.DMA((count + 1, 2)),
        ],
        compiler_params=PARAMS,
        cost_estimate=cost(2 * count * rows * width * cols, 2 * count * width * (rows + cols)),
    )(places, own, other, *early)
    return pl.pallas_call(
        down_last_kernel,
        in_specs=[VMEM] * 3,
        out_specs=VMEM,
        out_shape=jax.ShapeDtypeStruct(shape, jnp.bfloat16),
        scratch_shapes=[pltpu.VMEM((rows, cols), jnp.float32)],
        compiler_params=PARAMS,
        cost_estimate=cost(2 * rows * width * cols, 2 * width * (rows + cols)),
    )(late, *sums)


def around(block, axis):
    size = lax.axis_size(axis)
    before, after, blocks = block, block, [block]
    for distance in range(1, size // 2 + 1):
        before = shift(before, axis, 1)
        blocks.append(before)
        if distance < size - distance:
            after = shift(after, axis, size - 1)
            blocks.append(after)
    return blocks


def body(
    queries,
    key_cache,
    value_cache,
    new_key,
    new_value,
    lengths,
    residual,
    norm_gain,
    routes,
    route_weights,
    w_gate_up,
    w_down,
):
    n_x, n_tp, n_exp = lax.axis_size("x"), lax.axis_size("tp"), lax.axis_size("exp")

    attn_out, packed, picker = attend_and_pack(
        lengths,
        routes.T,
        route_weights.T,
        [queries, new_key, new_value, residual, key_cache, value_cache],
        n_x,
    )
    _, _, capacity, part = packed.shape
    packed = packed.reshape(n_x * n_exp, capacity, part)
    packed, w_gate_up, w_down = lax.optimization_barrier((packed, w_gate_up, w_down))
    gate_up_own, down_own = jnp.moveaxis(w_gate_up[0], 1, 0), w_down[0]
    gate_up_other, down_other = shift(gate_up_own, "core", 1), shift(down_own, "core", 1)
    arrived = lax.all_to_all(packed, ("x", "exp"), split_axis=0, concat_axis=0, tiled=True)
    arrived = arrived.reshape(n_x * n_exp * capacity, part)

    distance = jnp.array([0, -1, 1, -2, 2, -3, 3, 4], jnp.int32)
    places = (lax.axis_index("tp") + distance) % n_tp
    blocks = around(arrived, "tp")
    units = expert_units(blocks, places, norm_gain[None, :], gate_up_own, gate_up_other)
    blocks = around(units, "tp")
    shape = (n_x * n_exp, capacity, part)
    partial = expert_outputs(blocks, places, down_own, down_other, shape)

    returned = lax.all_to_all(partial, ("x", "exp"), split_axis=0, concat_axis=0, tiled=True)
    outputs = returned.reshape(n_x * n_exp * capacity, part).astype(jnp.float32)
    moe_out = lax.dot_general(
        picker, outputs, (((0,), (0,)), ((), ())), precision=lax.Precision.HIGHEST
    ).astype(jnp.bfloat16)
    return (attn_out, moe_out)


def solution(mesh):
    sizes = mesh.shape
    cores = 2
    chips = Mesh(
        mesh.devices.reshape(sizes["attn"] // cores, cores, sizes["tp"], sizes["exp"]),
        ("x", "core", "tp", "exp"),
    )
    rows = ("x", "core", "exp")
    return jax.shard_map(
        body,
        mesh=chips,
        in_specs=(
            P(rows, "tp"),
            P(rows, "tp", None, None),
            P(rows, "tp", None, None),
            P(rows, "tp"),
            P(rows, "tp"),
            P(rows),
            P(rows, "tp"),
            P(),
            P(rows, None),
            P(rows, None),
            P("exp", None, None, ("x", "core", "tp")),
            P("exp", ("x", "core"), "tp"),
        ),
        out_specs=(P(rows, "tp"), P(rows, "tp")),
        check_vma=False,
    )
```

time: 203 us -> 152 us (0.75)
  waiting for transfers between devices: 79.8 us -> 32.6 us
  starting transfers between devices: 35.5 us -> 55.7 us
  local copies, waits for them, and re-layouts: 18.9 us -> 4.11 us
  blocking collectives: 30 us -> 43.4 us
  between operations: 14.3 us -> 0.91 us
  matrix products: 10.9 us -> 0.95 us
  Pallas kernels: 6.21 us -> 13.4 us
  other arithmetic: 6.37 us -> 0.01 us
    all_gather x1 -> x0, waiting for transfers between devices: 45.2 us -> none  [body(): gathered = lax.all_gather(units, 'tp', axis=0, tiled=True)]
    ppermute x5 -> x16, starting transfers between devices: 15.3 us -> 55.7 us  [shift(): lax.ppermute(value, axis, [(i, (i + step) % size) for i in range(size)])]
    all_to_all x2 -> x0, starting transfers between devices: 20.2 us -> none  [the longest x1 10.3 us: body(): lax.all_to_all(copies, 'tp', split_axis=0, concat_axis=0, tiled=True)]
    all_to_all x2 -> x0, waiting for transfers between devices: 13.5 us -> none  [the longest x1 13.5 us: body(): lax.all_to_all(partial, ('x', 'exp'), split_axis=0, concat_axis=0, tiled=...]
    all_to_all x1 -> x2, blocking collectives: 30 us -> 43.4 us  [the longest x1 25.5 us: body(): lax.all_to_all(packed, ('x', 'exp'), split_axis=0, concat_axis=0, tiled=T...]
    ppermute x5 -> x16, waiting for transfers between devices: 21.1 us -> 32.6 us  [shift(): lax.ppermute(value, axis, [(i, (i + step) % size) for i in range(size)])]
    dot_general x7 -> x1, matrix products: 10.9 us -> 0.95 us  [body(): lax.dot_general(picker, outputs, (((0,), (0,)), ((), ())), precision=lax....]
    unnamed x14 -> x4, local copies, waits for them, and re-layouts: 7.83 us -> 0.01 us
  transfers between devices with their start and end apart: 8 -> 16, of which waited for: 5 -> 8; matrix products, arithmetic and copies ran while one was open for 10% -> 0% of each run, Pallas kernels for 0% -> 7%
where the time goes in v2:
time: 152 us; the launch traced here: 151 us
  starting transfers between devices  55.7 us (37%)
  blocking collectives  43.4 us (29%)
  waiting for transfers between devices  32.6 us (21%)
  Pallas kernels  13.4 us (9%)
  local copies, waits for them, and re-layouts  4.11 us (3%)
    ppermute x16, starting transfers between devices, shift(): lax.ppermute(value, axis, [(i, (i + step) % size) for i in range(size)])  55.7 us
    ppermute x16, waiting for transfers between devices, shift(): lax.ppermute(value, axis, [(i, (i + step) % size) for i in range(size)])  32.6 us
    all_to_all x1, blocking collectives, body(): lax.all_to_all(packed, ('x', 'exp'), split_axis=0, concat_axis=0, tiled=T...  25.5 us
    all_to_all x1, blocking collectives, body(): lax.all_to_all(partial, ('x', 'exp'), split_axis=0, concat_axis=0, tiled=...  17.9 us
    pallas_call x1, Pallas kernels, expert_units(): pl.pallas_call(functools.partial(up_first_kernel, count), in_specs=[SMEM,...  5.4 us
    optimization_barrier x1, local copies, waits for them, and re-layouts, body(): lax.optimization_barrier((packed, w_gate_up, w_down))  3.96 us
    pallas_call x1, Pallas kernels, expert_outputs(): pl.pallas_call(functools.partial(down_first_kernel, count), in_specs=[SME...  3.64 us
  transfers between devices with their start and end apart: 16, of which 8 were waited for; matrix products, arithmetic and copies ran while one was open for 0% of the time, Pallas kernels for 7%

profile of v2, /device:TPU:8, one launch (start us, length us, event | category | flops | bytes accessed | tf_op | source)
XLA Modules:
  0.0 151.1 jit_solution(12051899477866112709)
XLA Ops:
  0.6 2.8 %shard_map.140 = (bf16[24,384]{1,0:T(8,128)(2,1)}, bf16[4,8,12,384]{3,2,1,0:T(8,128)(2,1)S(1)}, f32[384,24]{1,0:T(8,128)S(1)}) custom-call(s32[24]{0:T(128)} %refs_0_.1, s32[2,24]{1,0:T(2,128)} %bitcast.17, f32[2,24]{1,0:T(2,128)} %bitcast.18, bf16[24,384]{1,0:T(8,128)(2,1)} %refs_3_.1, bf16[24,128]{1,0:T(8,128)(2,1)} %refs_4_.1, bf16[24,128]{1,0:T(8,128)(2,1)} %refs_5_.1, ...), custom_call_target="tpu_custom_call" | custom-call | tf_op jit(solution)/shard_map/pallas_call | solution.py:108
  3.5 4.0 %copy.18 = bf16[1,3072,2,256]{3,1,2,0:T(8,128)(2,1)} copy(bf16[1,3072,2,256]{3,2,1,0:T(2,128)(2,1)} %param.23) | data formatting | bytes 6291456 | tf_op jit(solution)/shard_map/optimization_barrier | solution.py:345
  7.4 1.9 %collective-permute-start.4 = (bf16[2,3072,256]{2,1,0:T(8,128)(2,1)}, bf16[2,3072,256]{2,1,0:T(8,128)(2,1)}, u32[]{:S(2)}, u32[]{:S(2)}) collective-permute-start(bf16[2,3072,256]{2,1,0:T(8,128)(2,1)} %bitcast.11.own_ref), channel_id=1, source_target_pairs={{0,64},{64,0},{1,65},{65,1},{2,66},{66,2},{3,67},{67,3},{4,68},{68... | collective-permute-start | bytes 9437192 | tf_op jit(solution)/shard_map/ppermute | solution.py:133
  9.3 25.5 %all_to_all.10 = bf16[32,12,384]{2,1,0:T(8,128)(2,1)S(1)} all-to-all(bf16[32,12,384]{2,1,0:T(8,128)(2,1)S(1)} %bitcast.12), channel_id=1, replica_groups=mesh['x'=4,'core'=2,'tp'=8,'exp'=8] {'x','exp'}, dimensions={0} | all-to-all | bytes 589824 | tf_op jit(solution)/shard_map/all_to_all | solution.py:348
  34.9 4.3 %collective-permute-start = (bf16[384,384]{1,0:T(8,128)(2,1)S(1)}, bf16[384,384]{1,0:T(8,128)(2,1)S(1)}, u32[]{:S(2)}, u32[]{:S(2)}) collective-permute-start(bf16[384,384]{1,0:T(8,128)(2,1)S(1)} %reshape.14.refs_0_), channel_id=1, source_target_pairs={{0,8},{8,16},{16,24},{24,32},{32,40},{40,48},{48,56},{56,0},{1,9},... | collective-permute-start | bytes 884744 | tf_op jit(solution)/shard_map/ppermute | solution.py:133
  39.2 8.6 %collective-permute-start.5 = (bf16[384,384]{1,0:T(8,128)(2,1)S(1)}, bf16[384,384]{1,0:T(8,128)(2,1)S(1)}, u32[]{:S(2)}, u32[]{:S(2)}) collective-permute-start(bf16[384,384]{1,0:T(8,128)(2,1)S(1)} %reshape.14.refs_0_), channel_id=1, source_target_pairs={{0,56},{8,0},{16,8},{24,16},{32,24},{40,32},{48,40},{56,48},{1,57}... | collective-permute-start | bytes 884744 | tf_op jit(solution)/shard_map/ppermute | solution.py:133
  47.8 4.1 %collective-permute-done.refs_1_ = bf16[384,384]{1,0:T(8,128)(2,1)S(1)} collective-permute-done((bf16[384,384]{1,0:T(8,128)(2,1)S(1)}, bf16[384,384]{1,0:T(8,128)(2,1)S(1)}, u32[]{:S(2)}, u32[]{:S(2)}) %collective-permute-start) | collective-permute-done | bytes 294944 | tf_op jit(solution)/shard_map/ppermute | solution.py:133
  51.9 1.9 %collective-permute-start.1 = (bf16[384,384]{1,0:T(8,128)(2,1)S(1)}, bf16[384,384]{1,0:T(8,128)(2,1)S(1)}, u32[]{:S(2)}, u32[]{:S(2)}) collective-permute-start(bf16[384,384]{1,0:T(8,128)(2,1)S(1)} %collective-permute-done.refs_1_), channel_id=1, source_target_pairs={{0,8},{8,16},{16,24},{24,32},{32,40},{40,48},{48,56},{56,0},{1,9},... | collective-permute-start | bytes 884744 | tf_op jit(solution)/shard_map/ppermute | solution.py:133
  53.8 5.1 %collective-permute-start.6 = (bf16[384,384]{1,0:T(8,128)(2,1)S(1)}, bf16[384,384]{1,0:T(8,128)(2,1)S(1)}, u32[]{:S(2)}, u32[]{:S(2)}) collective-permute-start(bf16[384,384]{1,0:T(8,128)(2,1)S(1)} %collective-permute-done.5.refs_2_), channel_id=1, source_target_pairs={{0,56},{8,0},{16,8},{24,16},{32,24},{40,32},{48,40},{56,48},{1,57}... | collective-permute-start | bytes 884744 | tf_op jit(solution)/shard_map/ppermute | solution.py:133
  59.0 3.2 %collective-permute-done.1.refs_3_ = bf16[384,384]{1,0:T(8,128)(2,1)S(1)} collective-permute-done((bf16[384,384]{1,0:T(8,128)(2,1)S(1)}, bf16[384,384]{1,0:T(8,128)(2,1)S(1)}, u32[]{:S(2)}, u32[]{:S(2)}) %collective-permute-start.1) | collective-permute-done | bytes 294944 | tf_op jit(solution)/shard_map/ppermute | solution.py:133
  64.1 5.1 %collective-permute-start.7 = (bf16[384,384]{1,0:T(8,128)(2,1)S(1)}, bf16[384,384]{1,0:T(8,128)(2,1)S(1)}, u32[]{:S(2)}, u32[]{:S(2)}) collective-permute-start(bf16[384,384]{1,0:T(8,128)(2,1)S(1)} %collective-permute-done.6.refs_4_), channel_id=1, source_target_pairs={{0,56},{8,0},{16,8},{24,16},{32,24},{40,32},{48,40},{56,48},{1,57}... | collective-permute-start | bytes 884744 | tf_op jit(solution)/shard_map/ppermute | solution.py:133
  69.2 1.9 %collective-permute-start.12 = (bf16[2048,384]{1,0:T(8,128)(2,1)}, bf16[2048,384]{1,0:T(8,128)(2,1)}, u32[]{:S(2)}, u32[]{:S(2)}) collective-permute-start(bf16[2048,384]{1,0:T(8,128)(2,1)} %bitcast.15), channel_id=1, source_target_pairs={{0,64},{64,0},{1,65},{65,1},{2,66},{66,2},{3,67},{67,3},{4,68},{68... | collective-permute-start | bytes 4718600 | tf_op jit(solution)/shard_map/ppermute | solution.py:133
  73.9 5.4 %shard_map.141 = (f32[4,384,256]{2,1,0:T(8,128)S(1)}, f32[384,128]{1,0:T(8,128)S(1)}, bf16[2,2,384,256]{3,2,1,0:T(8,128)(2,1)S(1)}) custom-call(s32[8]{0:T(128)S(1)} %and_select_fusion.place_ref, f32[1,3072]{1,0:T(1,128)S(1)} %bitcast.13, bf16[2,3072,256]{2,1,0:T(8,128)(2,1)} %bitcast.11.own_ref, bf16[2,3072,256]{2,1,0:T(8,128)(2,1)} %collective-permute-done.4.other_ref, ...), custom_call_target="tpu_custom_call" | custom-call | flops 2113929216 | bytes 5505024 | tf_op jit(solution)/shard_map/pallas_call | solution.py:249
  79.3 4.3 %collective-permute-done.3.row_ref = bf16[384,384]{1,0:T(8,128)(2,1)S(1)} collective-permute-done((bf16[384,384]{1,0:T(8,128)(2,1)S(1)}, bf16[384,384]{1,0:T(8,128)(2,1)S(1)}, u32[]{:S(2)}, u32[]{:S(2)}) %collective-permute-start.3) | collective-permute-done | bytes 294944 | tf_op jit(solution)/shard_map/ppermute | solution.py:133
  84.9 1.9 %collective-permute-start.8 = (bf16[384,512]{1,0:T(8,128)(2,1)S(1)}, bf16[384,512]{1,0:T(8,128)(2,1)S(1)}, u32[]{:S(2)}, u32[]{:S(2)}) collective-permute-start(bf16[384,512]{1,0:T(8,128)(2,1)S(1)} %shard_map.142.refs_0_), channel_id=1, source_target_pairs={{0,8},{8,16},{16,24},{24,32},{32,40},{40,48},{48,56},{56,0},{1,9},... | collective-permute-start | bytes 1179656 | tf_op jit(solution)/shard_map/ppermute | solution.py:133
  86.8 5.1 %collective-permute-start.13 = (bf16[384,512]{1,0:T(8,128)(2,1)S(1)}, bf16[384,512]{1,0:T(8,128)(2,1)S(1)}, u32[]{:S(2)}, u32[]{:S(2)}) collective-permute-start(bf16[384,512]{1,0:T(8,128)(2,1)S(1)} %shard_map.142.refs_0_), channel_id=1, source_target_pairs={{0,56},{8,0},{16,8},{24,16},{32,24},{40,32},{48,40},{56,48},{1,57}... | collective-permute-start | bytes 1179656 | tf_op jit(solution)/shard_map/ppermute | solution.py:133
  92.0 5.9 %collective-permute-done.8.refs_1_ = bf16[384,512]{1,0:T(8,128)(2,1)S(1)} collective-permute-done((bf16[384,512]{1,0:T(8,128)(2,1)S(1)}, bf16[384,512]{1,0:T(8,128)(2,1)S(1)}, u32[]{:S(2)}, u32[]{:S(2)}) %collective-permute-start.8) | collective-permute-done | bytes 393248 | tf_op jit(solution)/shard_map/ppermute | solution.py:133
  99.8 5.1 %collective-permute-start.14 = (bf16[384,512]{1,0:T(8,128)(2,1)S(1)}, bf16[384,512]{1,0:T(8,128)(2,1)S(1)}, u32[]{:S(2)}, u32[]{:S(2)}) collective-permute-start(bf16[384,512]{1,0:T(8,128)(2,1)S(1)} %collective-permute-done.13.refs_2_), channel_id=1, source_target_pairs={{0,56},{8,0},{16,8},{24,16},{32,24},{40,32},{48,40},{56,48},{1,57}... | collective-permute-start | bytes 1179656 | tf_op jit(solution)/shard_map/ppermute | solution.py:133
  104.9 4.9 %collective-permute-done.9.refs_3_ = bf16[384,512]{1,0:T(8,128)(2,1)S(1)} collective-permute-done((bf16[384,512]{1,0:T(8,128)(2,1)S(1)}, bf16[384,512]{1,0:T(8,128)(2,1)S(1)}, u32[]{:S(2)}, u32[]{:S(2)}) %collective-permute-start.9) | collective-permute-done | bytes 393248 | tf_op jit(solution)/shard_map/ppermute | solution.py:133
  111.8 5.1 %collective-permute-start.15 = (bf16[384,512]{1,0:T(8,128)(2,1)S(1)}, bf16[384,512]{1,0:T(8,128)(2,1)S(1)}, u32[]{:S(2)}, u32[]{:S(2)}) collective-permute-start(bf16[384,512]{1,0:T(8,128)(2,1)S(1)} %collective-permute-done.14.refs_4_), channel_id=1, source_target_pairs={{0,56},{8,0},{16,8},{24,16},{32,24},{40,32},{48,40},{56,48},{1,57}... | collective-permute-start | bytes 1179656 | tf_op jit(solution)/shard_map/ppermute | solution.py:133
  116.9 4.0 %collective-permute-done.10.refs_5_ = bf16[384,512]{1,0:T(8,128)(2,1)S(1)} collective-permute-done((bf16[384,512]{1,0:T(8,128)(2,1)S(1)}, bf16[384,512]{1,0:T(8,128)(2,1)S(1)}, u32[]{:S(2)}, u32[]{:S(2)}) %collective-permute-start.10) | collective-permute-done | bytes 393248 | tf_op jit(solution)/shard_map/ppermute | solution.py:133
  122.9 3.6 %shard_map.143 = (f32[384,384]{1,0:T(8,128)S(1)}, bf16[2,256,384]{2,1,0:T(8,128)(2,1)S(1)}) custom-call(s32[8]{0:T(128)S(1)} %and_select_fusion.place_ref, bf16[2048,384]{1,0:T(8,128)(2,1)} %bitcast.16, bf16[2048,384]{1,0:T(8,128)(2,1)} %collective-permute-done.12.other_ref, bf16[384,512]{1,0:T(8,128)(2,1)S(1)} %shard_map.142.refs_0_, ...), custom_call_target="tpu_custom_call" | custom-call | flops 1056964608 | bytes 5505024 | tf_op jit(solution)/shard_map/pallas_call | solution.py:282
  126.5 5.3 %collective-permute-done.11.unit_ref = bf16[384,512]{1,0:T(8,128)(2,1)S(1)} collective-permute-done((bf16[384,512]{1,0:T(8,128)(2,1)S(1)}, bf16[384,512]{1,0:T(8,128)(2,1)S(1)}, u32[]{:S(2)}, u32[]{:S(2)}) %collective-permute-start.11) | collective-permute-done | bytes 393248 | tf_op jit(solution)/shard_map/ppermute | solution.py:133
  132.2 17.9 %all_to_all.11 = bf16[32,12,384]{2,1,0:T(8,128)(2,1)S(1)} all-to-all(bf16[32,12,384]{2,1,0:T(8,128)(2,1)S(1)} %shard_map.144), channel_id=1, replica_groups=mesh['x'=4,'core'=2,'tp'=8,'exp'=8] {'x','exp'}, dimensions={0} | all-to-all | bytes 589824 | tf_op jit(solution)/shard_map/all_to_all | solution.py:359
  (24 shorter events, 13.1 us)
Async XLA Ops:
  3.4 70.5 %copy-start.1 = (s32[8]{0:T(128)S(1)}, s32[8]{0:T(128)}, u32[]{:S(2)}) copy-start(s32[8]{0:T(128)} %constant.22.clone) | copy-start | bytes 100
  3.4 70.5 %copy-start = (f32[3072]{0:T(1024)S(1)}, f32[3072]{0:T(1024)}, u32[]{:S(2)}) copy-start(f32[3072]{0:T(1024)} %param.20) | copy-start | bytes 36868
  7.4 66.5 %collective-permute-start.4 = (bf16[2,3072,256]{2,1,0:T(8,128)(2,1)}, bf16[2,3072,256]{2,1,0:T(8,128)(2,1)}, u32[]{:S(2)}, u32[]{:S(2)}) collective-permute-start(bf16[2,3072,256]{2,1,0:T(8,128)(2,1)} %bitcast.11.own_ref), channel_id=1, source_target_pairs={{0,64},{64,0},{1,65},{65,1},{2,66},{66,2},{3,67},{67,3},{4,68},{68... | collective-permute-start | bytes 9437192 | tf_op jit(solution)/shard_map/ppermute | solution.py:133
  34.9 17.0 %collective-permute-start = (bf16[384,384]{1,0:T(8,128)(2,1)S(1)}, bf16[384,384]{1,0:T(8,128)(2,1)S(1)}, u32[]{:S(2)}, u32[]{:S(2)}) collective-permute-start(bf16[384,384]{1,0:T(8,128)(2,1)S(1)} %reshape.14.refs_0_), channel_id=1, source_target_pairs={{0,8},{8,16},{16,24},{24,32},{32,40},{40,48},{48,56},{56,0},{1,9},... | collective-permute-start | bytes 884744 | tf_op jit(solution)/shard_map/ppermute | solution.py:133
  39.2 14.6 %collective-permute-start.5 = (bf16[384,384]{1,0:T(8,128)(2,1)S(1)}, bf16[384,384]{1,0:T(8,128)(2,1)S(1)}, u32[]{:S(2)}, u32[]{:S(2)}) collective-permute-start(bf16[384,384]{1,0:T(8,128)(2,1)S(1)} %reshape.14.refs_0_), channel_id=1, source_target_pairs={{0,56},{8,0},{16,8},{24,16},{32,24},{40,32},{48,40},{56,48},{1,57}... | collective-permute-start | bytes 884744 | tf_op jit(solution)/shard_map/ppermute | solution.py:133
  51.9 10.2 %collective-permute-start.1 = (bf16[384,384]{1,0:T(8,128)(2,1)S(1)}, bf16[384,384]{1,0:T(8,128)(2,1)S(1)}, u32[]{:S(2)}, u32[]{:S(2)}) collective-permute-start(bf16[384,384]{1,0:T(8,128)(2,1)S(1)} %collective-permute-done.refs_1_), channel_id=1, source_target_pairs={{0,8},{8,16},{16,24},{24,32},{32,40},{40,48},{48,56},{56,0},{1,9},... | collective-permute-start | bytes 884744 | tf_op jit(solution)/shard_map/ppermute | solution.py:133
  53.8 10.2 %collective-permute-start.6 = (bf16[384,384]{1,0:T(8,128)(2,1)S(1)}, bf16[384,384]{1,0:T(8,128)(2,1)S(1)}, u32[]{:S(2)}, u32[]{:S(2)}) collective-permute-start(bf16[384,384]{1,0:T(8,128)(2,1)S(1)} %collective-permute-done.5.refs_2_), channel_id=1, source_target_pairs={{0,56},{8,0},{16,8},{24,16},{32,24},{40,32},{48,40},{56,48},{1,57}... | collective-permute-start | bytes 884744 | tf_op jit(solution)/shard_map/ppermute | solution.py:133
  62.2 9.8 %collective-permute-start.2 = (bf16[384,384]{1,0:T(8,128)(2,1)S(1)}, bf16[384,384]{1,0:T(8,128)(2,1)S(1)}, u32[]{:S(2)}, u32[]{:S(2)}) collective-permute-start(bf16[384,384]{1,0:T(8,128)(2,1)S(1)} %collective-permute-done.1.refs_3_), channel_id=1, source_target_pairs={{0,8},{8,16},{16,24},{24,32},{32,40},{40,48},{48,56},{56,0},{1,9},... | collective-permute-start | bytes 884744 | tf_op jit(solution)/shard_map/ppermute | solution.py:133
  64.1 9.8 %collective-permute-start.7 = (bf16[384,384]{1,0:T(8,128)(2,1)S(1)}, bf16[384,384]{1,0:T(8,128)(2,1)S(1)}, u32[]{:S(2)}, u32[]{:S(2)}) collective-permute-start(bf16[384,384]{1,0:T(8,128)(2,1)S(1)} %collective-permute-done.6.refs_4_), channel_id=1, source_target_pairs={{0,56},{8,0},{16,8},{24,16},{32,24},{40,32},{48,40},{56,48},{1,57}... | collective-permute-start | bytes 884744 | tf_op jit(solution)/shard_map/ppermute | solution.py:133
  69.2 53.6 %collective-permute-start.12 = (bf16[2048,384]{1,0:T(8,128)(2,1)}, bf16[2048,384]{1,0:T(8,128)(2,1)}, u32[]{:S(2)}, u32[]{:S(2)}) collective-permute-start(bf16[2048,384]{1,0:T(8,128)(2,1)} %bitcast.15), channel_id=1, source_target_pairs={{0,64},{64,0},{1,65},{65,1},{2,66},{66,2},{3,67},{67,3},{4,68},{68... | collective-permute-start | bytes 4718600 | tf_op jit(solution)/shard_map/ppermute | solution.py:133
  72.0 11.7 %collective-permute-start.3 = (bf16[384,384]{1,0:T(8,128)(2,1)S(1)}, bf16[384,384]{1,0:T(8,128)(2,1)S(1)}, u32[]{:S(2)}, u32[]{:S(2)}) collective-permute-start(bf16[384,384]{1,0:T(8,128)(2,1)S(1)} %collective-permute-done.2.refs_5_), channel_id=1, source_target_pairs={{0,8},{8,16},{16,24},{24,32},{32,40},{40,48},{48,56},{56,0},{1,9},... | collective-permute-start | bytes 884744 | tf_op jit(solution)/shard_map/ppermute | solution.py:133
  84.9 12.9 %collective-permute-start.8 = (bf16[384,512]{1,0:T(8,128)(2,1)S(1)}, bf16[384,512]{1,0:T(8,128)(2,1)S(1)}, u32[]{:S(2)}, u32[]{:S(2)}) collective-permute-start(bf16[384,512]{1,0:T(8,128)(2,1)S(1)} %shard_map.142.refs_0_), channel_id=1, source_target_pairs={{0,8},{8,16},{16,24},{24,32},{32,40},{40,48},{48,56},{56,0},{1,9},... | collective-permute-start | bytes 1179656 | tf_op jit(solution)/shard_map/ppermute | solution.py:133
  86.8 12.9 %collective-permute-start.13 = (bf16[384,512]{1,0:T(8,128)(2,1)S(1)}, bf16[384,512]{1,0:T(8,128)(2,1)S(1)}, u32[]{:S(2)}, u32[]{:S(2)}) collective-permute-start(bf16[384,512]{1,0:T(8,128)(2,1)S(1)} %shard_map.142.refs_0_), channel_id=1, source_target_pairs={{0,56},{8,0},{16,8},{24,16},{32,24},{40,32},{48,40},{56,48},{1,57}... | collective-permute-start | bytes 1179656 | tf_op jit(solution)/shard_map/ppermute | solution.py:133
  97.8 12.0 %collective-permute-start.9 = (bf16[384,512]{1,0:T(8,128)(2,1)S(1)}, bf16[384,512]{1,0:T(8,128)(2,1)S(1)}, u32[]{:S(2)}, u32[]{:S(2)}) collective-permute-start(bf16[384,512]{1,0:T(8,128)(2,1)S(1)} %collective-permute-done.8.refs_1_), channel_id=1, source_target_pairs={{0,8},{8,16},{16,24},{24,32},{32,40},{40,48},{48,56},{56,0},{1,9},... | collective-permute-start | bytes 1179656 | tf_op jit(solution)/shard_map/ppermute | solution.py:133
  99.8 12.0 %collective-permute-start.14 = (bf16[384,512]{1,0:T(8,128)(2,1)S(1)}, bf16[384,512]{1,0:T(8,128)(2,1)S(1)}, u32[]{:S(2)}, u32[]{:S(2)}) collective-permute-start(bf16[384,512]{1,0:T(8,128)(2,1)S(1)} %collective-permute-done.13.refs_2_), channel_id=1, source_target_pairs={{0,56},{8,0},{16,8},{24,16},{32,24},{40,32},{48,40},{56,48},{1,57}... | collective-permute-start | bytes 1179656 | tf_op jit(solution)/shard_map/ppermute | solution.py:133
  109.8 11.1 %collective-permute-start.10 = (bf16[384,512]{1,0:T(8,128)(2,1)S(1)}, bf16[384,512]{1,0:T(8,128)(2,1)S(1)}, u32[]{:S(2)}, u32[]{:S(2)}) collective-permute-start(bf16[384,512]{1,0:T(8,128)(2,1)S(1)} %collective-permute-done.9.refs_3_), channel_id=1, source_target_pairs={{0,8},{8,16},{16,24},{24,32},{32,40},{40,48},{48,56},{56,0},{1,9},... | collective-permute-start | bytes 1179656 | tf_op jit(solution)/shard_map/ppermute | solution.py:133
  111.8 11.1 %collective-permute-start.15 = (bf16[384,512]{1,0:T(8,128)(2,1)S(1)}, bf16[384,512]{1,0:T(8,128)(2,1)S(1)}, u32[]{:S(2)}, u32[]{:S(2)}) collective-permute-start(bf16[384,512]{1,0:T(8,128)(2,1)S(1)} %collective-permute-done.14.refs_4_), channel_id=1, source_target_pairs={{0,56},{8,0},{16,8},{24,16},{32,24},{40,32},{48,40},{56,48},{1,57}... | collective-permute-start | bytes 1179656 | tf_op jit(solution)/shard_map/ppermute | solution.py:133
  120.9 10.9 %collective-permute-start.11 = (bf16[384,512]{1,0:T(8,128)(2,1)S(1)}, bf16[384,512]{1,0:T(8,128)(2,1)S(1)}, u32[]{:S(2)}, u32[]{:S(2)}) collective-permute-start(bf16[384,512]{1,0:T(8,128)(2,1)S(1)} %collective-permute-done.10.refs_5_), channel_id=1, source_target_pairs={{0,8},{8,16},{16,24},{24,32},{32,40},{40,48},{48,56},{56,0},{1,9},... | collective-permute-start | bytes 1179656 | tf_op jit(solution)/shard_map/ppermute | solution.py:133

commit v3 on v2

--- a/solution.py
+++ b/solution.py
@@ -140,8 +140,9 @@
         part = pl.ds(pl.multiple_of(places[index] * width, width), width)
         group = []
         for source, ref in enumerate(sources):
-            rows = ref.at[:, part] if len(ref.shape) == 3 else ref.at[part]
-            group.append(pltpu.make_async_copy(rows, target.at[source], sems.at[index, source]))
+            group.append(
+                pltpu.make_async_copy(ref.at[part], target.at[source], sems.at[index, source])
+            )
             group[-1].start()
         copies.append(group)
     return copies
@@ -155,7 +156,7 @@
     square = sum(square[:, lane : lane + HD] for lane in range(0, depth, HD))
     scaled = (rows * gain_ref[:, part]).astype(jnp.bfloat16)
     products = [
-        jnp.dot(scaled, weights[index // 2, index % 2], preferred_element_type=jnp.float32)
+        jnp.dot(scaled, weights[index], preferred_element_type=jnp.float32)
         for index in range(4)
     ]
     if total is None:
@@ -163,10 +164,11 @@
     return [old + new for old, new in zip(total, products)], squares + square
 
 
-def up_first_kernel(count, place_ref, gain_ref, own_ref, other_ref, *refs):
-    row_refs, (total_ref, squares_ref, ahead_ref, weights, sems) = refs[:count], refs[-5:]
+def up_first_kernel(count, place_ref, gain_ref, *refs):
+    source_refs, row_refs = refs[:4], refs[4 : 4 + count]
+    total_ref, squares_ref, ahead_ref, weights, sems = refs[-5:]
     scratch = [weights.at[index] for index in range(count)] + [ahead_ref]
-    copies = fetch((own_ref, other_ref), place_ref, scratch, sems)
+    copies = fetch(source_refs, place_ref, scratch, sems)
     total = squares = None
     for index, row_ref in enumerate(row_refs):
         for copy in copies[index]:
@@ -182,7 +184,7 @@
 
 
 def up_last_kernel(place_ref, gain_ref, row_ref, so_far_ref, squares_ref, weights_ref, out_ref):
-    width = weights_ref.shape[3]
+    width = weights_ref.shape[2]
     features = gain_ref.shape[1]
     place = place_ref[place_ref.shape[0] - 1]
     so_far = [so_far_ref[index] for index in range(4)]
@@ -239,16 +241,15 @@
     )
 
 
-def expert_units(blocks, places, gain, own, other):
-    (rows, depth), width = blocks[0].shape, own.shape[2]
-    own = pltpu.with_memory_space_constraint(own, pltpu.HBM)
-    other = pltpu.with_memory_space_constraint(other, pltpu.HBM)
+def expert_units(blocks, places, gain, sources):
+    (rows, depth), width = blocks[0].shape, sources[0].shape[1]
+    sources = [pltpu.with_memory_space_constraint(source, pltpu.HBM) for source in sources]
     *early, late = blocks
     count = len(early)
-    weights = (2, 2, depth, width)
+    weights = (4, depth, width)
     sums = pl.pallas_call(
         functools.partial(up_first_kernel, count),
-        in_specs=[SMEM, VMEM, HBM, HBM] + [VMEM] * count,
+        in_specs=[SMEM, VMEM] + [HBM] * 4 + [VMEM] * count,
         out_specs=[VMEM] * 3,
         out_shape=[
             jax.ShapeDtypeStruct((4, rows, width), jnp.float32),
@@ -257,11 +258,11 @@
         ],
         scratch_shapes=[
             pltpu.VMEM((count,) + weights, jnp.bfloat16),
-            pltpu.SemaphoreType.DMA((count + 1, 2)),
+            pltpu.SemaphoreType.DMA((count + 1, 4)),
         ],
         compiler_params=PARAMS,
         cost_estimate=cost(8 * count * rows * depth * width, 8 * count * depth * width),
-    )(places, gain, own, other, *early)
+    )(places, gain, *sources, *early)
     return pl.pallas_call(
         up_last_kernel,
         in_specs=[SMEM] + [VMEM] * 5,
@@ -343,15 +344,18 @@
     _, _, capacity, part = packed.shape
     packed = packed.reshape(n_x * n_exp, capacity, part)
     packed, w_gate_up, w_down = lax.optimization_barrier((packed, w_gate_up, w_down))
-    gate_up_own, down_own = jnp.moveaxis(w_gate_up[0], 1, 0), w_down[0]
-    gate_up_other, down_other = shift(gate_up_own, "core", 1), shift(down_own, "core", 1)
+    gate_own, up_own, down_own = w_gate_up[0, :, 0], w_gate_up[0, :, 1], w_down[0]
+    gate_other, up_other, down_other = (
+        shift(weights, "core", 1) for weights in (gate_own, up_own, down_own)
+    )
     arrived = lax.all_to_all(packed, ("x", "exp"), split_axis=0, concat_axis=0, tiled=True)
     arrived = arrived.reshape(n_x * n_exp * capacity, part)
 
     distance = jnp.array([0, -1, 1, -2, 2, -3, 3, 4], jnp.int32)
     places = (lax.axis_index("tp") + distance) % n_tp
     blocks = around(arrived, "tp")
-    units = expert_units(blocks, places, norm_gain[None, :], gate_up_own, gate_up_other)
+    sources = (gate_own, up_own, gate_other, up_other)
+    units = expert_units(blocks, places, norm_gain[None, :], sources)
     blocks = around(units, "tp")
     shape = (n_x * n_exp, capacity, part)
     partial = expert_outputs(blocks, places, down_own, down_other, shape)

time: 152 us -> 145 us (0.954)
  blocking collectives: 43.4 us -> 18.9 us
  starting transfers between devices: 55.7 us -> 68.3 us
  waiting for transfers between devices: 32.6 us -> 37.3 us
    all_to_all x1 -> x0, blocking collectives: 25.5 us -> none  [body(): lax.all_to_all(packed, ('x', 'exp'), split_axis=0, concat_axis=0, tiled=T...]
    all_to_all x0 -> x1, starting transfers between devices: none -> 10.2 us  [body(): lax.all_to_all(packed, ('x', 'exp'), split_axis=0, concat_axis=0, tiled=T...]
    all_to_all x0 -> x1, waiting for transfers between devices: none -> 6.38 us  [body(): lax.all_to_all(packed, ('x', 'exp'), split_axis=0, concat_axis=0, tiled=T...]
    ppermute x16 -> x17, starting transfers between devices: 55.7 us -> 58.1 us  [shift(): lax.ppermute(value, axis, [(i, (i + step) % size) for i in range(size)])]
    squeeze x0 -> x1, local copies, waits for them, and re-layouts: none -> 1.84 us  [body(): w_gate_up[0, :, 1]]
    optimization_barrier x1, local copies, waits for them, and re-layouts: 3.96 us -> 2.3 us  [body(): lax.optimization_barrier((packed, w_gate_up, w_down))]
    ppermute x16 -> x17, waiting for transfers between devices: 32.6 us -> 31 us  [shift(): lax.ppermute(value, axis, [(i, (i + step) % size) for i in range(size)])]
  transfers between devices with their start and end apart: 16 -> 18, of which waited for: 8 -> 9; matrix products, arithmetic and copies ran while one was open for 0% -> 3% of each run, Pallas kernels for 7% -> 7%
where the time goes in v3:
time: 145 us
  starting transfers between devices  68.3 us (47%)
  waiting for transfers between devices  37.3 us (26%)
  blocking collectives  18.9 us (13%)
  Pallas kernels  14 us (10%)
  local copies, waits for them, and re-layouts  4.29 us (3%)
    ppermute x17, starting transfers between devices, shift(): lax.ppermute(value, axis, [(i, (i + step) % size) for i in range(size)])  58.1 us
    ppermute x17, waiting for transfers between devices, shift(): lax.ppermute(value, axis, [(i, (i + step) % size) for i in range(size)])  31 us
    all_to_all x1, blocking collectives, body(): lax.all_to_all(partial, ('x', 'exp'), split_axis=0, concat_axis=0, tiled=...  18.9 us
    all_to_all x1, starting transfers between devices, body(): lax.all_to_all(packed, ('x', 'exp'), split_axis=0, concat_axis=0, tiled=T...  10.2 us
    all_to_all x1, waiting for transfers between devices, body(): lax.all_to_all(packed, ('x', 'exp'), split_axis=0, concat_axis=0, tiled=T...  6.38 us
    pallas_call x1, Pallas kernels, expert_units(): pl.pallas_call(functools.partial(up_first_kernel, count), in_specs=[SMEM,...  5.67 us
    pallas_call x1, Pallas kernels, expert_outputs(): pl.pallas_call(functools.partial(down_first_kernel, count), in_specs=[SME...  3.64 us
    pallas_call x1, Pallas kernels, attend_and_pack(): pl.pallas_call(front_kernel, in_specs=[pl.BlockSpec(memory_space=pltpu.HB...  3.09 us
  transfers between devices with their start and end apart: 18, of which 9 were waited for; matrix products, arithmetic and copies ran while one was open for 3% of the time, Pallas kernels for 7%

profile of v3, /device:TPU:8, one launch (start us, length us, event | category | flops | bytes accessed | tf_op | source)
XLA Modules:
  0.0 144.7 jit_solution(17586369607997489998)
XLA Ops:
  0.6 3.1 %shard_map.140 = (bf16[24,384]{1,0:T(8,128)(2,1)}, bf16[4,8,12,384]{3,2,1,0:T(8,128)(2,1)}, f32[384,24]{1,0:T(8,128)S(1)}) custom-call(s32[24]{0:T(128)} %refs_0_.1, s32[2,24]{1,0:T(2,128)} %bitcast.15, f32[2,24]{1,0:T(2,128)} %bitcast.16, bf16[24,384]{1,0:T(8,128)(2,1)} %refs_3_.1, bf16[24,128]{1,0:T(8,128)(2,1)} %refs_4_.1, bf16[24,128]{1,0:T(8,128)(2,1)} %refs_5_.1, ...), custom_call_target="tpu_custom_call" | custom-call | tf_op jit(solution)/shard_map/pallas_call | solution.py:108
  3.7 10.2 %all-to-all-start = ((bf16[32,12,384]{2,1,0:T(8,128)(2,1)}), bf16[32,12,384]{2,1,0:T(8,128)(2,1)S(1)}, u32[]{:S(2)}, u32[]{:S(2)}) async-start(bf16[32,12,384]{2,1,0:T(8,128)(2,1)} %bitcast.3), calls=%async_computation | async-start | bytes 786432 | tf_op jit(solution)/shard_map/all_to_all | solution.py:351
  13.9 2.3 %copy.17 = bf16[1,3072,2,256]{3,1,2,0:T(8,128)(2,1)S(1)} copy(bf16[1,3072,2,256]{3,2,1,0:T(2,128)(2,1)} %param.23) | data formatting | bytes 6291456 | tf_op jit(solution)/shard_map/optimization_barrier | solution.py:346
  20.0 2.4 %collective-permute-start.5 = (bf16[3072,256]{1,0:T(8,128)(2,1)}, bf16[3072,256]{1,0:T(8,128)(2,1)}, u32[]{:S(2)}, u32[]{:S(2)}) collective-permute-start(bf16[3072,256]{1,0:T(8,128)(2,1)} %get-tuple-element.24.refs_1_), channel_id=1, source_target_pairs={{0,64},{64,0},{1,65},{65,1},{2,66},{66,2},{3,67},{67,3},{4,68},{68... | collective-permute-start | bytes 4718600 | tf_op jit(solution)/shard_map/ppermute | solution.py:133
  22.4 6.4 %all-to-all-done = bf16[32,12,384]{2,1,0:T(8,128)(2,1)S(1)} async-done(((bf16[32,12,384]{2,1,0:T(8,128)(2,1)}), bf16[32,12,384]{2,1,0:T(8,128)(2,1)S(1)}, u32[]{:S(2)}, u32[]{:S(2)}) %all-to-all-start) | async-done | bytes 294944 | tf_op jit(solution)/shard_map/all_to_all | solution.py:351
  28.9 4.3 %collective-permute-start = (bf16[384,384]{1,0:T(8,128)(2,1)S(1)}, bf16[384,384]{1,0:T(8,128)(2,1)S(1)}, u32[]{:S(2)}, u32[]{:S(2)}) collective-permute-start(bf16[384,384]{1,0:T(8,128)(2,1)S(1)} %reshape.14.refs_4_), channel_id=1, source_target_pairs={{0,8},{8,16},{16,24},{24,32},{32,40},{40,48},{48,56},{56,0},{1,9},... | collective-permute-start | bytes 884744 | tf_op jit(solution)/shard_map/ppermute | solution.py:133
  33.2 8.6 %collective-permute-start.6 = (bf16[384,384]{1,0:T(8,128)(2,1)S(1)}, bf16[384,384]{1,0:T(8,128)(2,1)S(1)}, u32[]{:S(2)}, u32[]{:S(2)}) collective-permute-start(bf16[384,384]{1,0:T(8,128)(2,1)S(1)} %reshape.14.refs_4_), channel_id=1, source_target_pairs={{0,56},{8,0},{16,8},{24,16},{32,24},{40,32},{48,40},{56,48},{1,57}... | collective-permute-start | bytes 884744 | tf_op jit(solution)/shard_map/ppermute | solution.py:133
  41.8 3.2 %collective-permute-done.refs_5_ = bf16[384,384]{1,0:T(8,128)(2,1)S(1)} collective-permute-done((bf16[384,384]{1,0:T(8,128)(2,1)S(1)}, bf16[384,384]{1,0:T(8,128)(2,1)S(1)}, u32[]{:S(2)}, u32[]{:S(2)}) %collective-permute-start) | collective-permute-done | bytes 294944 | tf_op jit(solution)/shard_map/ppermute | solution.py:133
  46.9 5.1 %collective-permute-start.7 = (bf16[384,384]{1,0:T(8,128)(2,1)S(1)}, bf16[384,384]{1,0:T(8,128)(2,1)S(1)}, u32[]{:S(2)}, u32[]{:S(2)}) collective-permute-start(bf16[384,384]{1,0:T(8,128)(2,1)S(1)} %collective-permute-done.6.refs_6_), channel_id=1, source_target_pairs={{0,56},{8,0},{16,8},{24,16},{32,24},{40,32},{48,40},{56,48},{1,57}... | collective-permute-start | bytes 884744 | tf_op jit(solution)/shard_map/ppermute | solution.py:133
  52.1 2.7 %collective-permute-done.1.refs_7_ = bf16[384,384]{1,0:T(8,128)(2,1)S(1)} collective-permute-done((bf16[384,384]{1,0:T(8,128)(2,1)S(1)}, bf16[384,384]{1,0:T(8,128)(2,1)S(1)}, u32[]{:S(2)}, u32[]{:S(2)}) %collective-permute-start.1) | collective-permute-done | bytes 294944 | tf_op jit(solution)/shard_map/ppermute | solution.py:133
  56.7 5.1 %collective-permute-start.8 = (bf16[384,384]{1,0:T(8,128)(2,1)S(1)}, bf16[384,384]{1,0:T(8,128)(2,1)S(1)}, u32[]{:S(2)}, u32[]{:S(2)}) collective-permute-start(bf16[384,384]{1,0:T(8,128)(2,1)S(1)} %collective-permute-done.7.refs_8_), channel_id=1, source_target_pairs={{0,56},{8,0},{16,8},{24,16},{32,24},{40,32},{48,40},{56,48},{1,57}... | collective-permute-start | bytes 884744 | tf_op jit(solution)/shard_map/ppermute | solution.py:133
  61.9 1.9 %collective-permute-start.13 = (bf16[2048,384]{1,0:T(8,128)(2,1)}, bf16[2048,384]{1,0:T(8,128)(2,1)}, u32[]{:S(2)}, u32[]{:S(2)}) collective-permute-start(bf16[2048,384]{1,0:T(8,128)(2,1)} %bitcast.13), channel_id=1, source_target_pairs={{0,64},{64,0},{1,65},{65,1},{2,66},{66,2},{3,67},{67,3},{4,68},{68... | collective-permute-start | bytes 4718600 | tf_op jit(solution)/shard_map/ppermute | solution.py:133
  66.6 5.7 %shard_map.141 = (f32[4,384,256]{2,1,0:T(8,128)S(1)}, f32[384,128]{1,0:T(8,128)S(1)}, bf16[4,384,256]{2,1,0:T(8,128)(2,1)S(1)}) custom-call(s32[8]{0:T(128)S(1)} %and_select_fusion.place_ref, f32[1,3072]{1,0:T(1,128)S(1)} %bitcast.11, bf16[3072,256]{1,0:T(8,128)(2,1)} %get-tuple-element.25.refs_0_, bf16[3072,256]{1,0:T(8,128)(2,1)} %get-tuple-element.24.refs_1_, ...), custom_call_target="tpu_custom_call" | custom-call | flops 2113929216 | bytes 5505024 | tf_op jit(solution)/shard_map/pallas_call | solution.py:250
  72.3 4.1 %collective-permute-done.3.row_ref = bf16[384,384]{1,0:T(8,128)(2,1)S(1)} collective-permute-done((bf16[384,384]{1,0:T(8,128)(2,1)S(1)}, bf16[384,384]{1,0:T(8,128)(2,1)S(1)}, u32[]{:S(2)}, u32[]{:S(2)}) %collective-permute-start.3) | collective-permute-done | bytes 294944 | tf_op jit(solution)/shard_map/ppermute | solution.py:133
  77.5 1.9 %collective-permute-start.9 = (bf16[384,512]{1,0:T(8,128)(2,1)S(1)}, bf16[384,512]{1,0:T(8,128)(2,1)S(1)}, u32[]{:S(2)}, u32[]{:S(2)}) collective-permute-start(bf16[384,512]{1,0:T(8,128)(2,1)S(1)} %shard_map.142.refs_0_), channel_id=1, source_target_pairs={{0,8},{8,16},{16,24},{24,32},{32,40},{40,48},{48,56},{56,0},{1,9},... | collective-permute-start | bytes 1179656 | tf_op jit(solution)/shard_map/ppermute | solution.py:133
  79.5 5.1 %collective-permute-start.14 = (bf16[384,512]{1,0:T(8,128)(2,1)S(1)}, bf16[384,512]{1,0:T(8,128)(2,1)S(1)}, u32[]{:S(2)}, u32[]{:S(2)}) collective-permute-start(bf16[384,512]{1,0:T(8,128)(2,1)S(1)} %shard_map.142.refs_0_), channel_id=1, source_target_pairs={{0,56},{8,0},{16,8},{24,16},{32,24},{40,32},{48,40},{56,48},{1,57}... | collective-permute-start | bytes 1179656 | tf_op jit(solution)/shard_map/ppermute | solution.py:133
  84.6 5.9 %collective-permute-done.9.refs_1_ = bf16[384,512]{1,0:T(8,128)(2,1)S(1)} collective-permute-done((bf16[384,512]{1,0:T(8,128)(2,1)S(1)}, bf16[384,512]{1,0:T(8,128)(2,1)S(1)}, u32[]{:S(2)}, u32[]{:S(2)}) %collective-permute-start.9) | collective-permute-done | bytes 393248 | tf_op jit(solution)/shard_map/ppermute | solution.py:133
  92.4 5.1 %collective-permute-start.15 = (bf16[384,512]{1,0:T(8,128)(2,1)S(1)}, bf16[384,512]{1,0:T(8,128)(2,1)S(1)}, u32[]{:S(2)}, u32[]{:S(2)}) collective-permute-start(bf16[384,512]{1,0:T(8,128)(2,1)S(1)} %collective-permute-done.14.refs_2_), channel_id=1, source_target_pairs={{0,56},{8,0},{16,8},{24,16},{32,24},{40,32},{48,40},{56,48},{1,57}... | collective-permute-start | bytes 1179656 | tf_op jit(solution)/shard_map/ppermute | solution.py:133
  97.6 4.9 %collective-permute-done.10.refs_3_ = bf16[384,512]{1,0:T(8,128)(2,1)S(1)} collective-permute-done((bf16[384,512]{1,0:T(8,128)(2,1)S(1)}, bf16[384,512]{1,0:T(8,128)(2,1)S(1)}, u32[]{:S(2)}, u32[]{:S(2)}) %collective-permute-start.10) | collective-permute-done | bytes 393248 | tf_op jit(solution)/shard_map/ppermute | solution.py:133
  104.4 5.1 %collective-permute-start.16 = (bf16[384,512]{1,0:T(8,128)(2,1)S(1)}, bf16[384,512]{1,0:T(8,128)(2,1)S(1)}, u32[]{:S(2)}, u32[]{:S(2)}) collective-permute-start(bf16[384,512]{1,0:T(8,128)(2,1)S(1)} %collective-permute-done.15.refs_4_), channel_id=1, source_target_pairs={{0,56},{8,0},{16,8},{24,16},{32,24},{40,32},{48,40},{56,48},{1,57}... | collective-permute-start | bytes 1179656 | tf_op jit(solution)/shard_map/ppermute | solution.py:133
  109.6 4.0 %collective-permute-done.11.refs_5_ = bf16[384,512]{1,0:T(8,128)(2,1)S(1)} collective-permute-done((bf16[384,512]{1,0:T(8,128)(2,1)S(1)}, bf16[384,512]{1,0:T(8,128)(2,1)S(1)}, u32[]{:S(2)}, u32[]{:S(2)}) %collective-permute-start.11) | collective-permute-done | bytes 393248 | tf_op jit(solution)/shard_map/ppermute | solution.py:133
  115.5 3.6 %shard_map.143 = (f32[384,384]{1,0:T(8,128)S(1)}, bf16[2,256,384]{2,1,0:T(8,128)(2,1)S(1)}) custom-call(s32[8]{0:T(128)S(1)} %and_select_fusion.place_ref, bf16[2048,384]{1,0:T(8,128)(2,1)} %bitcast.14, bf16[2048,384]{1,0:T(8,128)(2,1)} %collective-permute-done.13.other_ref, bf16[384,512]{1,0:T(8,128)(2,1)S(1)} %shard_map.142.refs_0_, ...), custom_call_target="tpu_custom_call" | custom-call | flops 1056964608 | bytes 5505024 | tf_op jit(solution)/shard_map/pallas_call | solution.py:283
  119.2 5.3 %collective-permute-done.12.unit_ref = bf16[384,512]{1,0:T(8,128)(2,1)S(1)} collective-permute-done((bf16[384,512]{1,0:T(8,128)(2,1)S(1)}, bf16[384,512]{1,0:T(8,128)(2,1)S(1)}, u32[]{:S(2)}, u32[]{:S(2)}) %collective-permute-start.12) | collective-permute-done | bytes 393248 | tf_op jit(solution)/shard_map/ppermute | solution.py:133
  124.8 18.9 %all_to_all.10 = bf16[32,12,384]{2,1,0:T(8,128)(2,1)S(1)} all-to-all(bf16[32,12,384]{2,1,0:T(8,128)(2,1)S(1)} %shard_map.144), channel_id=1, replica_groups=mesh['x'=4,'core'=2,'tp'=8,'exp'=8] {'x','exp'}, dimensions={0} | all-to-all | bytes 589824 | tf_op jit(solution)/shard_map/all_to_all | solution.py:363
  (28 shorter events, 18.8 us)
Async XLA Ops:
  3.7 25.1 %all-to-all-start = ((bf16[32,12,384]{2,1,0:T(8,128)(2,1)}), bf16[32,12,384]{2,1,0:T(8,128)(2,1)S(1)}, u32[]{:S(2)}, u32[]{:S(2)}) async-start(bf16[32,12,384]{2,1,0:T(8,128)(2,1)} %bitcast.3), calls=%async_computation | async-start | bytes 786432 | tf_op jit(solution)/shard_map/all_to_all | solution.py:351
  16.2 50.3 %copy-start.1 = (s32[8]{0:T(128)S(1)}, s32[8]{0:T(128)}, u32[]{:S(2)}) copy-start(s32[8]{0:T(128)} %constant.22.clone) | copy-start | bytes 100
  16.2 50.4 %copy-start = (f32[3072]{0:T(1024)S(1)}, f32[3072]{0:T(1024)}, u32[]{:S(2)}) copy-start(f32[3072]{0:T(1024)} %param.20) | copy-start | bytes 36868
  18.1 48.5 %collective-permute-start.4 = (bf16[3072,256]{1,0:T(8,128)(2,1)}, bf16[3072,256]{1,0:T(8,128)(2,1)}, u32[]{:S(2)}, u32[]{:S(2)}) collective-permute-start(bf16[3072,256]{1,0:T(8,128)(2,1)} %get-tuple-element.25.refs_0_), channel_id=1, source_target_pairs={{0,64},{64,0},{1,65},{65,1},{2,66},{66,2},{3,67},{67,3},{4,68},{68... | collective-permute-start | bytes 4718600 | tf_op jit(solution)/shard_map/ppermute | solution.py:133
  20.0 46.6 %collective-permute-start.5 = (bf16[3072,256]{1,0:T(8,128)(2,1)}, bf16[3072,256]{1,0:T(8,128)(2,1)}, u32[]{:S(2)}, u32[]{:S(2)}) collective-permute-start(bf16[3072,256]{1,0:T(8,128)(2,1)} %get-tuple-element.24.refs_1_), channel_id=1, source_target_pairs={{0,64},{64,0},{1,65},{65,1},{2,66},{66,2},{3,67},{67,3},{4,68},{68... | collective-permute-start | bytes 4718600 | tf_op jit(solution)/shard_map/ppermute | solution.py:133
  28.9 16.1 %collective-permute-start = (bf16[384,384]{1,0:T(8,128)(2,1)S(1)}, bf16[384,384]{1,0:T(8,128)(2,1)S(1)}, u32[]{:S(2)}, u32[]{:S(2)}) collective-permute-start(bf16[384,384]{1,0:T(8,128)(2,1)S(1)} %reshape.14.refs_4_), channel_id=1, source_target_pairs={{0,8},{8,16},{16,24},{24,32},{32,40},{40,48},{48,56},{56,0},{1,9},... | collective-permute-start | bytes 884744 | tf_op jit(solution)/shard_map/ppermute | solution.py:133
  33.2 13.7 %collective-permute-start.6 = (bf16[384,384]{1,0:T(8,128)(2,1)S(1)}, bf16[384,384]{1,0:T(8,128)(2,1)S(1)}, u32[]{:S(2)}, u32[]{:S(2)}) collective-permute-start(bf16[384,384]{1,0:T(8,128)(2,1)S(1)} %reshape.14.refs_4_), channel_id=1, source_target_pairs={{0,56},{8,0},{16,8},{24,16},{32,24},{40,32},{48,40},{56,48},{1,57}... | collective-permute-start | bytes 884744 | tf_op jit(solution)/shard_map/ppermute | solution.py:133
  45.0 9.8 %collective-permute-start.1 = (bf16[384,384]{1,0:T(8,128)(2,1)S(1)}, bf16[384,384]{1,0:T(8,128)(2,1)S(1)}, u32[]{:S(2)}, u32[]{:S(2)}) collective-permute-start(bf16[384,384]{1,0:T(8,128)(2,1)S(1)} %collective-permute-done.refs_5_), channel_id=1, source_target_pairs={{0,8},{8,16},{16,24},{24,32},{32,40},{40,48},{48,56},{56,0},{1,9},... | collective-permute-start | bytes 884744 | tf_op jit(solution)/shard_map/ppermute | solution.py:133
  46.9 9.8 %collective-permute-start.7 = (bf16[384,384]{1,0:T(8,128)(2,1)S(1)}, bf16[384,384]{1,0:T(8,128)(2,1)S(1)}, u32[]{:S(2)}, u32[]{:S(2)}) collective-permute-start(bf16[384,384]{1,0:T(8,128)(2,1)S(1)} %collective-permute-done.6.refs_6_), channel_id=1, source_target_pairs={{0,56},{8,0},{16,8},{24,16},{32,24},{40,32},{48,40},{56,48},{1,57}... | collective-permute-start | bytes 884744 | tf_op jit(solution)/shard_map/ppermute | solution.py:133
  54.8 9.8 %collective-permute-start.2 = (bf16[384,384]{1,0:T(8,128)(2,1)S(1)}, bf16[384,384]{1,0:T(8,128)(2,1)S(1)}, u32[]{:S(2)}, u32[]{:S(2)}) collective-permute-start(bf16[384,384]{1,0:T(8,128)(2,1)S(1)} %collective-permute-done.1.refs_7_), channel_id=1, source_target_pairs={{0,8},{8,16},{16,24},{24,32},{32,40},{40,48},{48,56},{56,0},{1,9},... | collective-permute-start | bytes 884744 | tf_op jit(solution)/shard_map/ppermute | solution.py:133
  56.7 9.8 %collective-permute-start.8 = (bf16[384,384]{1,0:T(8,128)(2,1)S(1)}, bf16[384,384]{1,0:T(8,128)(2,1)S(1)}, u32[]{:S(2)}, u32[]{:S(2)}) collective-permute-start(bf16[384,384]{1,0:T(8,128)(2,1)S(1)} %collective-permute-done.7.refs_8_), channel_id=1, source_target_pairs={{0,56},{8,0},{16,8},{24,16},{32,24},{40,32},{48,40},{56,48},{1,57}... | collective-permute-start | bytes 884744 | tf_op jit(solution)/shard_map/ppermute | solution.py:133
  61.9 53.6 %collective-permute-start.13 = (bf16[2048,384]{1,0:T(8,128)(2,1)}, bf16[2048,384]{1,0:T(8,128)(2,1)}, u32[]{:S(2)}, u32[]{:S(2)}) collective-permute-start(bf16[2048,384]{1,0:T(8,128)(2,1)} %bitcast.13), channel_id=1, source_target_pairs={{0,64},{64,0},{1,65},{65,1},{2,66},{66,2},{3,67},{67,3},{4,68},{68... | collective-permute-start | bytes 4718600 | tf_op jit(solution)/shard_map/ppermute | solution.py:133
  64.6 11.7 %collective-permute-start.3 = (bf16[384,384]{1,0:T(8,128)(2,1)S(1)}, bf16[384,384]{1,0:T(8,128)(2,1)S(1)}, u32[]{:S(2)}, u32[]{:S(2)}) collective-permute-start(bf16[384,384]{1,0:T(8,128)(2,1)S(1)} %collective-permute-done.2.refs_9_), channel_id=1, source_target_pairs={{0,8},{8,16},{16,24},{24,32},{32,40},{40,48},{48,56},{56,0},{1,9},... | collective-permute-start | bytes 884744 | tf_op jit(solution)/shard_map/ppermute | solution.py:133
  77.5 12.9 %collective-permute-start.9 = (bf16[384,512]{1,0:T(8,128)(2,1)S(1)}, bf16[384,512]{1,0:T(8,128)(2,1)S(1)}, u32[]{:S(2)}, u32[]{:S(2)}) collective-permute-start(bf16[384,512]{1,0:T(8,128)(2,1)S(1)} %shard_map.142.refs_0_), channel_id=1, source_target_pairs={{0,8},{8,16},{16,24},{24,32},{32,40},{40,48},{48,56},{56,0},{1,9},... | collective-permute-start | bytes 1179656 | tf_op jit(solution)/shard_map/ppermute | solution.py:133
  79.5 12.9 %collective-permute-start.14 = (bf16[384,512]{1,0:T(8,128)(2,1)S(1)}, bf16[384,512]{1,0:T(8,128)(2,1)S(1)}, u32[]{:S(2)}, u32[]{:S(2)}) collective-permute-start(bf16[384,512]{1,0:T(8,128)(2,1)S(1)} %shard_map.142.refs_0_), channel_id=1, source_target_pairs={{0,56},{8,0},{16,8},{24,16},{32,24},{40,32},{48,40},{56,48},{1,57}... | collective-permute-start | bytes 1179656 | tf_op jit(solution)/shard_map/ppermute | solution.py:133
  90.5 12.0 %collective-permute-start.10 = (bf16[384,512]{1,0:T(8,128)(2,1)S(1)}, bf16[384,512]{1,0:T(8,128)(2,1)S(1)}, u32[]{:S(2)}, u32[]{:S(2)}) collective-permute-start(bf16[384,512]{1,0:T(8,128)(2,1)S(1)} %collective-permute-done.9.refs_1_), channel_id=1, source_target_pairs={{0,8},{8,16},{16,24},{24,32},{32,40},{40,48},{48,56},{56,0},{1,9},... | collective-permute-start | bytes 1179656 | tf_op jit(solution)/shard_map/ppermute | solution.py:133
  92.4 12.0 %collective-permute-start.15 = (bf16[384,512]{1,0:T(8,128)(2,1)S(1)}, bf16[384,512]{1,0:T(8,128)(2,1)S(1)}, u32[]{:S(2)}, u32[]{:S(2)}) collective-permute-start(bf16[384,512]{1,0:T(8,128)(2,1)S(1)} %collective-permute-done.14.refs_2_), channel_id=1, source_target_pairs={{0,56},{8,0},{16,8},{24,16},{32,24},{40,32},{48,40},{56,48},{1,57}... | collective-permute-start | bytes 1179656 | tf_op jit(solution)/shard_map/ppermute | solution.py:133
  102.5 11.1 %collective-permute-start.11 = (bf16[384,512]{1,0:T(8,128)(2,1)S(1)}, bf16[384,512]{1,0:T(8,128)(2,1)S(1)}, u32[]{:S(2)}, u32[]{:S(2)}) collective-permute-start(bf16[384,512]{1,0:T(8,128)(2,1)S(1)} %collective-permute-done.10.refs_3_), channel_id=1, source_target_pairs={{0,8},{8,16},{16,24},{24,32},{32,40},{40,48},{48,56},{56,0},{1,9},... | collective-permute-start | bytes 1179656 | tf_op jit(solution)/shard_map/ppermute | solution.py:133
  104.4 11.1 %collective-permute-start.16 = (bf16[384,512]{1,0:T(8,128)(2,1)S(1)}, bf16[384,512]{1,0:T(8,128)(2,1)S(1)}, u32[]{:S(2)}, u32[]{:S(2)}) collective-permute-start(bf16[384,512]{1,0:T(8,128)(2,1)S(1)} %collective-permute-done.15.refs_4_), channel_id=1, source_target_pairs={{0,56},{8,0},{16,8},{24,16},{32,24},{40,32},{48,40},{56,48},{1,57}... | collective-permute-start | bytes 1179656 | tf_op jit(solution)/shard_map/ppermute | solution.py:133
  113.6 10.9 %collective-permute-start.12 = (bf16[384,512]{1,0:T(8,128)(2,1)S(1)}, bf16[384,512]{1,0:T(8,128)(2,1)S(1)}, u32[]{:S(2)}, u32[]{:S(2)}) collective-permute-start(bf16[384,512]{1,0:T(8,128)(2,1)S(1)} %collective-permute-done.11.refs_5_), channel_id=1, source_target_pairs={{0,8},{8,16},{16,24},{24,32},{32,40},{40,48},{48,56},{56,0},{1,9},... | collective-permute-start | bytes 1179656 | tf_op jit(solution)/shard_map/ppermute | solution.py:133

commit v4 on v3

--- a/solution.py
+++ b/solution.py
@@ -50,8 +50,7 @@
         chosen = (slot_ids == target).astype(jnp.float32)
         placement = placement + chosen
         picker = picker + route_weights_ref[k : k + 1] * chosen
-    for copy in range(copy_count):
-        picker_ref[copy * slot_total : (copy + 1) * slot_total] = picker
+    picker_ref[...] = picker
 
     for copy in copies[3:]:
         copy.wait()
@@ -112,7 +111,7 @@
         out_shape=[
             jax.ShapeDtypeStruct((row_count, part), jnp.bfloat16),
             jax.ShapeDtypeStruct((copy_count, EXPERTS, capacity, part), jnp.bfloat16),
-            jax.ShapeDtypeStruct((copy_count * slot_total, row_count), jnp.float32),
+            jax.ShapeDtypeStruct((slot_total, row_count), jnp.float32),
         ],
         scratch_shapes=[pltpu.SMEM(lengths.shape, lengths.dtype)]
         + [pltpu.VMEM(value.shape, value.dtype) for value in tensors[1:]]
@@ -318,6 +317,35 @@
     return blocks
 
 
+def combine_kernel(picker_ref, parts_ref, out_ref, total_ref):
+    chips, experts, capacity, _ = parts_ref.shape
+    for expert in range(experts):
+        total = parts_ref[0, expert].astype(jnp.float32)
+        for chip in range(1, chips):
+            total = total + parts_ref[chip, expert].astype(jnp.float32)
+        total_ref[pl.ds(expert * capacity, capacity)] = total
+    picked = lax.dot_general(
+        picker_ref[...],
+        total_ref[...],
+        (((0,), (0,)), ((), ())),
+        precision=lax.Precision.HIGHEST,
+        preferred_element_type=jnp.float32,
+    )
+    out_ref[...] = picked.astype(out_ref.dtype)
+
+
+def combined(picker, parts):
+    (slots, rows), cols = picker.shape, parts.shape[3]
+    return pl.pallas_call(
+        combine_kernel,
+        in_specs=[VMEM] * 2,
+        out_specs=VMEM,
+        out_shape=jax.ShapeDtypeStruct((rows, cols), jnp.bfloat16),
+        scratch_shapes=[pltpu.VMEM((slots, cols), jnp.float32)],
+        compiler_params=PARAMS,
+    )(picker, parts)
+
+
 def body(
     queries,
     key_cache,
@@ -361,10 +389,7 @@
     partial = expert_outputs(blocks, places, down_own, down_other, shape)
 
     returned = lax.all_to_all(partial, ("x", "exp"), split_axis=0, concat_axis=0, tiled=True)
-    outputs = returned.reshape(n_x * n_exp * capacity, part).astype(jnp.float32)
-    moe_out = lax.dot_general(
-        picker, outputs, (((0,), (0,)), ((), ())), precision=lax.Precision.HIGHEST
-    ).astype(jnp.bfloat16)
+    moe_out = combined(picker, returned.reshape(n_x, n_exp, capacity, part))
     return (attn_out, moe_out)
 
 

time: 145 us -> 145 us (level)
  no operation moved by 1% of the time
where the time goes in v4:
time: 145 us
  starting transfers between devices  68.3 us (47%)
  waiting for transfers between devices  37.3 us (26%)
  blocking collectives  18.9 us (13%)
  Pallas kernels  14.9 us (10%)
  local copies, waits for them, and re-layouts  4.22 us (3%)
    ppermute x17, starting transfers between devices, shift(): lax.ppermute(value, axis, [(i, (i + step) % size) for i in range(size)])  58.1 us
    ppermute x17, waiting for transfers between devices, shift(): lax.ppermute(value, axis, [(i, (i + step) % size) for i in range(size)])  31 us
    all_to_all x1, blocking collectives, body(): lax.all_to_all(partial, ('x', 'exp'), split_axis=0, concat_axis=0, tiled=...  18.9 us
    all_to_all x1, starting transfers between devices, body(): lax.all_to_all(packed, ('x', 'exp'), split_axis=0, concat_axis=0, tiled=T...  10.2 us
    all_to_all x1, waiting for transfers between devices, body(): lax.all_to_all(packed, ('x', 'exp'), split_axis=0, concat_axis=0, tiled=T...  6.38 us
    pallas_call x1, Pallas kernels, expert_units(): pl.pallas_call(functools.partial(up_first_kernel, count), in_specs=[SMEM,...  5.67 us
    pallas_call x1, Pallas kernels, expert_outputs(): pl.pallas_call(functools.partial(down_first_kernel, count), in_specs=[SME...  3.64 us
    pallas_call x1, Pallas kernels, attend_and_pack(): pl.pallas_call(front_kernel, in_specs=[pl.BlockSpec(memory_space=pltpu.HB...  3.09 us
  transfers between devices with their start and end apart: 18, of which 9 were waited for; matrix products, arithmetic and copies ran while one was open for 3% of the time, Pallas kernels for 7%

profile of v4, /device:TPU:8, one launch (start us, length us, event | category | flops | bytes accessed | tf_op | source)
XLA Modules:
  0.0 144.6 jit_solution(12893434367760706328)
XLA Ops:
  0.6 3.1 %shard_map.140 = (bf16[24,384]{1,0:T(8,128)(2,1)}, bf16[4,8,12,384]{3,2,1,0:T(8,128)(2,1)}, f32[96,24]{1,0:T(8,128)S(1)}) custom-call(s32[24]{0:T(128)} %refs_0_.1, s32[2,24]{1,0:T(2,128)} %bitcast.15, f32[2,24]{1,0:T(2,128)} %bitcast.16, bf16[24,384]{1,0:T(8,128)(2,1)} %refs_3_.1, bf16[24,128]{1,0:T(8,128)(2,1)} %refs_4_.1, bf16[24,128]{1,0:T(8,128)(2,1)} %refs_5_.1, ...), custom_call_target="tpu_custom_call" | custom-call | tf_op jit(solution)/shard_map/pallas_call | solution.py:107
  3.7 10.2 %all-to-all-start = ((bf16[32,12,384]{2,1,0:T(8,128)(2,1)}), bf16[32,12,384]{2,1,0:T(8,128)(2,1)S(1)}, u32[]{:S(2)}, u32[]{:S(2)}) async-start(bf16[32,12,384]{2,1,0:T(8,128)(2,1)} %bitcast.3), calls=%async_computation | async-start | bytes 786432 | tf_op jit(solution)/shard_map/all_to_all | solution.py:379
  13.9 2.3 %copy.17 = bf16[1,3072,2,256]{3,1,2,0:T(8,128)(2,1)S(1)} copy(bf16[1,3072,2,256]{3,2,1,0:T(2,128)(2,1)} %param.23) | data formatting | bytes 6291456 | tf_op jit(solution)/shard_map/optimization_barrier | solution.py:374
  20.0 2.4 %collective-permute-start.5 = (bf16[3072,256]{1,0:T(8,128)(2,1)}, bf16[3072,256]{1,0:T(8,128)(2,1)}, u32[]{:S(2)}, u32[]{:S(2)}) collective-permute-start(bf16[3072,256]{1,0:T(8,128)(2,1)} %get-tuple-element.24.refs_1_), channel_id=1, source_target_pairs={{0,64},{64,0},{1,65},{65,1},{2,66},{66,2},{3,67},{67,3},{4,68},{68... | collective-permute-start | bytes 4718600 | tf_op jit(solution)/shard_map/ppermute | solution.py:132
  22.4 6.4 %all-to-all-done = bf16[32,12,384]{2,1,0:T(8,128)(2,1)S(1)} async-done(((bf16[32,12,384]{2,1,0:T(8,128)(2,1)}), bf16[32,12,384]{2,1,0:T(8,128)(2,1)S(1)}, u32[]{:S(2)}, u32[]{:S(2)}) %all-to-all-start) | async-done | bytes 294944 | tf_op jit(solution)/shard_map/all_to_all | solution.py:379
  28.9 4.3 %collective-permute-start = (bf16[384,384]{1,0:T(8,128)(2,1)S(1)}, bf16[384,384]{1,0:T(8,128)(2,1)S(1)}, u32[]{:S(2)}, u32[]{:S(2)}) collective-permute-start(bf16[384,384]{1,0:T(8,128)(2,1)S(1)} %reshape.14.refs_4_), channel_id=1, source_target_pairs={{0,8},{8,16},{16,24},{24,32},{32,40},{40,48},{48,56},{56,0},{1,9},... | collective-permute-start | bytes 884744 | tf_op jit(solution)/shard_map/ppermute | solution.py:132
  33.2 8.6 %collective-permute-start.6 = (bf16[384,384]{1,0:T(8,128)(2,1)S(1)}, bf16[384,384]{1,0:T(8,128)(2,1)S(1)}, u32[]{:S(2)}, u32[]{:S(2)}) collective-permute-start(bf16[384,384]{1,0:T(8,128)(2,1)S(1)} %reshape.14.refs_4_), channel_id=1, source_target_pairs={{0,56},{8,0},{16,8},{24,16},{32,24},{40,32},{48,40},{56,48},{1,57}... | collective-permute-start | bytes 884744 | tf_op jit(solution)/shard_map/ppermute | solution.py:132
  41.8 3.2 %collective-permute-done.refs_5_ = bf16[384,384]{1,0:T(8,128)(2,1)S(1)} collective-permute-done((bf16[384,384]{1,0:T(8,128)(2,1)S(1)}, bf16[384,384]{1,0:T(8,128)(2,1)S(1)}, u32[]{:S(2)}, u32[]{:S(2)}) %collective-permute-start) | collective-permute-done | bytes 294944 | tf_op jit(solution)/shard_map/ppermute | solution.py:132
  46.9 5.1 %collective-permute-start.7 = (bf16[384,384]{1,0:T(8,128)(2,1)S(1)}, bf16[384,384]{1,0:T(8,128)(2,1)S(1)}, u32[]{:S(2)}, u32[]{:S(2)}) collective-permute-start(bf16[384,384]{1,0:T(8,128)(2,1)S(1)} %collective-permute-done.6.refs_6_), channel_id=1, source_target_pairs={{0,56},{8,0},{16,8},{24,16},{32,24},{40,32},{48,40},{56,48},{1,57}... | collective-permute-start | bytes 884744 | tf_op jit(solution)/shard_map/ppermute | solution.py:132
  52.1 2.7 %collective-permute-done.1.refs_7_ = bf16[384,384]{1,0:T(8,128)(2,1)S(1)} collective-permute-done((bf16[384,384]{1,0:T(8,128)(2,1)S(1)}, bf16[384,384]{1,0:T(8,128)(2,1)S(1)}, u32[]{:S(2)}, u32[]{:S(2)}) %collective-permute-start.1) | collective-permute-done | bytes 294944 | tf_op jit(solution)/shard_map/ppermute | solution.py:132
  56.7 5.1 %collective-permute-start.8 = (bf16[384,384]{1,0:T(8,128)(2,1)S(1)}, bf16[384,384]{1,0:T(8,128)(2,1)S(1)}, u32[]{:S(2)}, u32[]{:S(2)}) collective-permute-start(bf16[384,384]{1,0:T(8,128)(2,1)S(1)} %collective-permute-done.7.refs_8_), channel_id=1, source_target_pairs={{0,56},{8,0},{16,8},{24,16},{32,24},{40,32},{48,40},{56,48},{1,57}... | collective-permute-start | bytes 884744 | tf_op jit(solution)/shard_map/ppermute | solution.py:132
  61.9 1.9 %collective-permute-start.13 = (bf16[2048,384]{1,0:T(8,128)(2,1)}, bf16[2048,384]{1,0:T(8,128)(2,1)}, u32[]{:S(2)}, u32[]{:S(2)}) collective-permute-start(bf16[2048,384]{1,0:T(8,128)(2,1)} %bitcast.13), channel_id=1, source_target_pairs={{0,64},{64,0},{1,65},{65,1},{2,66},{66,2},{3,67},{67,3},{4,68},{68... | collective-permute-start | bytes 4718600 | tf_op jit(solution)/shard_map/ppermute | solution.py:132
  66.6 5.7 %shard_map.141 = (f32[4,384,256]{2,1,0:T(8,128)S(1)}, f32[384,128]{1,0:T(8,128)S(1)}, bf16[4,384,256]{2,1,0:T(8,128)(2,1)S(1)}) custom-call(s32[8]{0:T(128)S(1)} %and_select_fusion.place_ref, f32[1,3072]{1,0:T(1,128)S(1)} %bitcast.11, bf16[3072,256]{1,0:T(8,128)(2,1)} %get-tuple-element.25.refs_0_, bf16[3072,256]{1,0:T(8,128)(2,1)} %get-tuple-element.24.refs_1_, ...), custom_call_target="tpu_custom_call" | custom-call | flops 2113929216 | bytes 5505024 | tf_op jit(solution)/shard_map/pallas_call | solution.py:249
  72.3 4.1 %collective-permute-done.3.row_ref = bf16[384,384]{1,0:T(8,128)(2,1)S(1)} collective-permute-done((bf16[384,384]{1,0:T(8,128)(2,1)S(1)}, bf16[384,384]{1,0:T(8,128)(2,1)S(1)}, u32[]{:S(2)}, u32[]{:S(2)}) %collective-permute-start.3) | collective-permute-done | bytes 294944 | tf_op jit(solution)/shard_map/ppermute | solution.py:132
  77.5 1.9 %collective-permute-start.9 = (bf16[384,512]{1,0:T(8,128)(2,1)S(1)}, bf16[384,512]{1,0:T(8,128)(2,1)S(1)}, u32[]{:S(2)}, u32[]{:S(2)}) collective-permute-start(bf16[384,512]{1,0:T(8,128)(2,1)S(1)} %shard_map.142.refs_0_), channel_id=1, source_target_pairs={{0,8},{8,16},{16,24},{24,32},{32,40},{40,48},{48,56},{56,0},{1,9},... | collective-permute-start | bytes 1179656 | tf_op jit(solution)/shard_map/ppermute | solution.py:132
  79.5 5.1 %collective-permute-start.14 = (bf16[384,512]{1,0:T(8,128)(2,1)S(1)}, bf16[384,512]{1,0:T(8,128)(2,1)S(1)}, u32[]{:S(2)}, u32[]{:S(2)}) collective-permute-start(bf16[384,512]{1,0:T(8,128)(2,1)S(1)} %shard_map.142.refs_0_), channel_id=1, source_target_pairs={{0,56},{8,0},{16,8},{24,16},{32,24},{40,32},{48,40},{56,48},{1,57}... | collective-permute-start | bytes 1179656 | tf_op jit(solution)/shard_map/ppermute | solution.py:132
  84.6 5.9 %collective-permute-done.9.refs_1_ = bf16[384,512]{1,0:T(8,128)(2,1)S(1)} collective-permute-done((bf16[384,512]{1,0:T(8,128)(2,1)S(1)}, bf16[384,512]{1,0:T(8,128)(2,1)S(1)}, u32[]{:S(2)}, u32[]{:S(2)}) %collective-permute-start.9) | collective-permute-done | bytes 393248 | tf_op jit(solution)/shard_map/ppermute | solution.py:132
  92.4 5.1 %collective-permute-start.15 = (bf16[384,512]{1,0:T(8,128)(2,1)S(1)}, bf16[384,512]{1,0:T(8,128)(2,1)S(1)}, u32[]{:S(2)}, u32[]{:S(2)}) collective-permute-start(bf16[384,512]{1,0:T(8,128)(2,1)S(1)} %collective-permute-done.14.refs_2_), channel_id=1, source_target_pairs={{0,56},{8,0},{16,8},{24,16},{32,24},{40,32},{48,40},{56,48},{1,57}... | collective-permute-start | bytes 1179656 | tf_op jit(solution)/shard_map/ppermute | solution.py:132
  97.6 4.9 %collective-permute-done.10.refs_3_ = bf16[384,512]{1,0:T(8,128)(2,1)S(1)} collective-permute-done((bf16[384,512]{1,0:T(8,128)(2,1)S(1)}, bf16[384,512]{1,0:T(8,128)(2,1)S(1)}, u32[]{:S(2)}, u32[]{:S(2)}) %collective-permute-start.10) | collective-permute-done | bytes 393248 | tf_op jit(solution)/shard_map/ppermute | solution.py:132
  104.4 5.1 %collective-permute-start.16 = (bf16[384,512]{1,0:T(8,128)(2,1)S(1)}, bf16[384,512]{1,0:T(8,128)(2,1)S(1)}, u32[]{:S(2)}, u32[]{:S(2)}) collective-permute-start(bf16[384,512]{1,0:T(8,128)(2,1)S(1)} %collective-permute-done.15.refs_4_), channel_id=1, source_target_pairs={{0,56},{8,0},{16,8},{24,16},{32,24},{40,32},{48,40},{56,48},{1,57}... | collective-permute-start | bytes 1179656 | tf_op jit(solution)/shard_map/ppermute | solution.py:132
  109.6 4.0 %collective-permute-done.11.refs_5_ = bf16[384,512]{1,0:T(8,128)(2,1)S(1)} collective-permute-done((bf16[384,512]{1,0:T(8,128)(2,1)S(1)}, bf16[384,512]{1,0:T(8,128)(2,1)S(1)}, u32[]{:S(2)}, u32[]{:S(2)}) %collective-permute-start.11) | collective-permute-done | bytes 393248 | tf_op jit(solution)/shard_map/ppermute | solution.py:132
  115.5 3.6 %shard_map.143 = (f32[384,384]{1,0:T(8,128)S(1)}, bf16[2,256,384]{2,1,0:T(8,128)(2,1)S(1)}) custom-call(s32[8]{0:T(128)S(1)} %and_select_fusion.place_ref, bf16[2048,384]{1,0:T(8,128)(2,1)} %bitcast.14, bf16[2048,384]{1,0:T(8,128)(2,1)} %collective-permute-done.13.other_ref, bf16[384,512]{1,0:T(8,128)(2,1)S(1)} %shard_map.142.refs_0_, ...), custom_call_target="tpu_custom_call" | custom-call | flops 1056964608 | bytes 5505024 | tf_op jit(solution)/shard_map/pallas_call | solution.py:282
  119.2 5.3 %collective-permute-done.12.unit_ref = bf16[384,512]{1,0:T(8,128)(2,1)S(1)} collective-permute-done((bf16[384,512]{1,0:T(8,128)(2,1)S(1)}, bf16[384,512]{1,0:T(8,128)(2,1)S(1)}, u32[]{:S(2)}, u32[]{:S(2)}) %collective-permute-start.12) | collective-permute-done | bytes 393248 | tf_op jit(solution)/shard_map/ppermute | solution.py:132
  124.8 18.9 %all_to_all.10 = bf16[32,12,384]{2,1,0:T(8,128)(2,1)S(1)} all-to-all(bf16[32,12,384]{2,1,0:T(8,128)(2,1)S(1)} %shard_map.144), channel_id=1, replica_groups=mesh['x'=4,'core'=2,'tp'=8,'exp'=8] {'x','exp'}, dimensions={0} | all-to-all | bytes 589824 | tf_op jit(solution)/shard_map/all_to_all | solution.py:391
  (27 shorter events, 18.6 us)
Async XLA Ops:
  3.7 25.1 %all-to-all-start = ((bf16[32,12,384]{2,1,0:T(8,128)(2,1)}), bf16[32,12,384]{2,1,0:T(8,128)(2,1)S(1)}, u32[]{:S(2)}, u32[]{:S(2)}) async-start(bf16[32,12,384]{2,1,0:T(8,128)(2,1)} %bitcast.3), calls=%async_computation | async-start | bytes 786432 | tf_op jit(solution)/shard_map/all_to_all | solution.py:379
  16.2 50.3 %copy-start.1 = (s32[8]{0:T(128)S(1)}, s32[8]{0:T(128)}, u32[]{:S(2)}) copy-start(s32[8]{0:T(128)} %constant.22.clone) | copy-start | bytes 100
  16.2 50.4 %copy-start = (f32[3072]{0:T(1024)S(1)}, f32[3072]{0:T(1024)}, u32[]{:S(2)}) copy-start(f32[3072]{0:T(1024)} %param.20) | copy-start | bytes 36868
  18.1 48.5 %collective-permute-start.4 = (bf16[3072,256]{1,0:T(8,128)(2,1)}, bf16[3072,256]{1,0:T(8,128)(2,1)}, u32[]{:S(2)}, u32[]{:S(2)}) collective-permute-start(bf16[3072,256]{1,0:T(8,128)(2,1)} %get-tuple-element.25.refs_0_), channel_id=1, source_target_pairs={{0,64},{64,0},{1,65},{65,1},{2,66},{66,2},{3,67},{67,3},{4,68},{68... | collective-permute-start | bytes 4718600 | tf_op jit(solution)/shard_map/ppermute | solution.py:132
  20.0 46.6 %collective-permute-start.5 = (bf16[3072,256]{1,0:T(8,128)(2,1)}, bf16[3072,256]{1,0:T(8,128)(2,1)}, u32[]{:S(2)}, u32[]{:S(2)}) collective-permute-start(bf16[3072,256]{1,0:T(8,128)(2,1)} %get-tuple-element.24.refs_1_), channel_id=1, source_target_pairs={{0,64},{64,0},{1,65},{65,1},{2,66},{66,2},{3,67},{67,3},{4,68},{68... | collective-permute-start | bytes 4718600 | tf_op jit(solution)/shard_map/ppermute | solution.py:132
  28.9 16.1 %collective-permute-start = (bf16[384,384]{1,0:T(8,128)(2,1)S(1)}, bf16[384,384]{1,0:T(8,128)(2,1)S(1)}, u32[]{:S(2)}, u32[]{:S(2)}) collective-permute-start(bf16[384,384]{1,0:T(8,128)(2,1)S(1)} %reshape.14.refs_4_), channel_id=1, source_target_pairs={{0,8},{8,16},{16,24},{24,32},{32,40},{40,48},{48,56},{56,0},{1,9},... | collective-permute-start | bytes 884744 | tf_op jit(solution)/shard_map/ppermute | solution.py:132
  33.2 13.7 %collective-permute-start.6 = (bf16[384,384]{1,0:T(8,128)(2,1)S(1)}, bf16[384,384]{1,0:T(8,128)(2,1)S(1)}, u32[]{:S(2)}, u32[]{:S(2)}) collective-permute-start(bf16[384,384]{1,0:T(8,128)(2,1)S(1)} %reshape.14.refs_4_), channel_id=1, source_target_pairs={{0,56},{8,0},{16,8},{24,16},{32,24},{40,32},{48,40},{56,48},{1,57}... | collective-permute-start | bytes 884744 | tf_op jit(solution)/shard_map/ppermute | solution.py:132
  45.0 9.8 %collective-permute-start.1 = (bf16[384,384]{1,0:T(8,128)(2,1)S(1)}, bf16[384,384]{1,0:T(8,128)(2,1)S(1)}, u32[]{:S(2)}, u32[]{:S(2)}) collective-permute-start(bf16[384,384]{1,0:T(8,128)(2,1)S(1)} %collective-permute-done.refs_5_), channel_id=1, source_target_pairs={{0,8},{8,16},{16,24},{24,32},{32,40},{40,48},{48,56},{56,0},{1,9},... | collective-permute-start | bytes 884744 | tf_op jit(solution)/shard_map/ppermute | solution.py:132
  46.9 9.8 %collective-permute-start.7 = (bf16[384,384]{1,0:T(8,128)(2,1)S(1)}, bf16[384,384]{1,0:T(8,128)(2,1)S(1)}, u32[]{:S(2)}, u32[]{:S(2)}) collective-permute-start(bf16[384,384]{1,0:T(8,128)(2,1)S(1)} %collective-permute-done.6.refs_6_), channel_id=1, source_target_pairs={{0,56},{8,0},{16,8},{24,16},{32,24},{40,32},{48,40},{56,48},{1,57}... | collective-permute-start | bytes 884744 | tf_op jit(solution)/shard_map/ppermute | solution.py:132
  54.8 9.8 %collective-permute-start.2 = (bf16[384,384]{1,0:T(8,128)(2,1)S(1)}, bf16[384,384]{1,0:T(8,128)(2,1)S(1)}, u32[]{:S(2)}, u32[]{:S(2)}) collective-permute-start(bf16[384,384]{1,0:T(8,128)(2,1)S(1)} %collective-permute-done.1.refs_7_), channel_id=1, source_target_pairs={{0,8},{8,16},{16,24},{24,32},{32,40},{40,48},{48,56},{56,0},{1,9},... | collective-permute-start | bytes 884744 | tf_op jit(solution)/shard_map/ppermute | solution.py:132
  56.7 9.8 %collective-permute-start.8 = (bf16[384,384]{1,0:T(8,128)(2,1)S(1)}, bf16[384,384]{1,0:T(8,128)(2,1)S(1)}, u32[]{:S(2)}, u32[]{:S(2)}) collective-permute-start(bf16[384,384]{1,0:T(8,128)(2,1)S(1)} %collective-permute-done.7.refs_8_), channel_id=1, source_target_pairs={{0,56},{8,0},{16,8},{24,16},{32,24},{40,32},{48,40},{56,48},{1,57}... | collective-permute-start | bytes 884744 | tf_op jit(solution)/shard_map/ppermute | solution.py:132
  61.9 53.6 %collective-permute-start.13 = (bf16[2048,384]{1,0:T(8,128)(2,1)}, bf16[2048,384]{1,0:T(8,128)(2,1)}, u32[]{:S(2)}, u32[]{:S(2)}) collective-permute-start(bf16[2048,384]{1,0:T(8,128)(2,1)} %bitcast.13), channel_id=1, source_target_pairs={{0,64},{64,0},{1,65},{65,1},{2,66},{66,2},{3,67},{67,3},{4,68},{68... | collective-permute-start | bytes 4718600 | tf_op jit(solution)/shard_map/ppermute | solution.py:132
  64.6 11.7 %collective-permute-start.3 = (bf16[384,384]{1,0:T(8,128)(2,1)S(1)}, bf16[384,384]{1,0:T(8,128)(2,1)S(1)}, u32[]{:S(2)}, u32[]{:S(2)}) collective-permute-start(bf16[384,384]{1,0:T(8,128)(2,1)S(1)} %collective-permute-done.2.refs_9_), channel_id=1, source_target_pairs={{0,8},{8,16},{16,24},{24,32},{32,40},{40,48},{48,56},{56,0},{1,9},... | collective-permute-start | bytes 884744 | tf_op jit(solution)/shard_map/ppermute | solution.py:132
  77.5 12.9 %collective-permute-start.9 = (bf16[384,512]{1,0:T(8,128)(2,1)S(1)}, bf16[384,512]{1,0:T(8,128)(2,1)S(1)}, u32[]{:S(2)}, u32[]{:S(2)}) collective-permute-start(bf16[384,512]{1,0:T(8,128)(2,1)S(1)} %shard_map.142.refs_0_), channel_id=1, source_target_pairs={{0,8},{8,16},{16,24},{24,32},{32,40},{40,48},{48,56},{56,0},{1,9},... | collective-permute-start | bytes 1179656 | tf_op jit(solution)/shard_map/ppermute | solution.py:132
  79.5 12.9 %collective-permute-start.14 = (bf16[384,512]{1,0:T(8,128)(2,1)S(1)}, bf16[384,512]{1,0:T(8,128)(2,1)S(1)}, u32[]{:S(2)}, u32[]{:S(2)}) collective-permute-start(bf16[384,512]{1,0:T(8,128)(2,1)S(1)} %shard_map.142.refs_0_), channel_id=1, source_target_pairs={{0,56},{8,0},{16,8},{24,16},{32,24},{40,32},{48,40},{56,48},{1,57}... | collective-permute-start | bytes 1179656 | tf_op jit(solution)/shard_map/ppermute | solution.py:132
  90.5 12.0 %collective-permute-start.10 = (bf16[384,512]{1,0:T(8,128)(2,1)S(1)}, bf16[384,512]{1,0:T(8,128)(2,1)S(1)}, u32[]{:S(2)}, u32[]{:S(2)}) collective-permute-start(bf16[384,512]{1,0:T(8,128)(2,1)S(1)} %collective-permute-done.9.refs_1_), channel_id=1, source_target_pairs={{0,8},{8,16},{16,24},{24,32},{32,40},{40,48},{48,56},{56,0},{1,9},... | collective-permute-start | bytes 1179656 | tf_op jit(solution)/shard_map/ppermute | solution.py:132
  92.4 12.0 %collective-permute-start.15 = (bf16[384,512]{1,0:T(8,128)(2,1)S(1)}, bf16[384,512]{1,0:T(8,128)(2,1)S(1)}, u32[]{:S(2)}, u32[]{:S(2)}) collective-permute-start(bf16[384,512]{1,0:T(8,128)(2,1)S(1)} %collective-permute-done.14.refs_2_), channel_id=1, source_target_pairs={{0,56},{8,0},{16,8},{24,16},{32,24},{40,32},{48,40},{56,48},{1,57}... | collective-permute-start | bytes 1179656 | tf_op jit(solution)/shard_map/ppermute | solution.py:132
  102.5 11.1 %collective-permute-start.11 = (bf16[384,512]{1,0:T(8,128)(2,1)S(1)}, bf16[384,512]{1,0:T(8,128)(2,1)S(1)}, u32[]{:S(2)}, u32[]{:S(2)}) collective-permute-start(bf16[384,512]{1,0:T(8,128)(2,1)S(1)} %collective-permute-done.10.refs_3_), channel_id=1, source_target_pairs={{0,8},{8,16},{16,24},{24,32},{32,40},{40,48},{48,56},{56,0},{1,9},... | collective-permute-start | bytes 1179656 | tf_op jit(solution)/shard_map/ppermute | solution.py:132
  104.4 11.1 %collective-permute-start.16 = (bf16[384,512]{1,0:T(8,128)(2,1)S(1)}, bf16[384,512]{1,0:T(8,128)(2,1)S(1)}, u32[]{:S(2)}, u32[]{:S(2)}) collective-permute-start(bf16[384,512]{1,0:T(8,128)(2,1)S(1)} %collective-permute-done.15.refs_4_), channel_id=1, source_target_pairs={{0,56},{8,0},{16,8},{24,16},{32,24},{40,32},{48,40},{56,48},{1,57}... | collective-permute-start | bytes 1179656 | tf_op jit(solution)/shard_map/ppermute | solution.py:132
  113.6 10.9 %collective-permute-start.12 = (bf16[384,512]{1,0:T(8,128)(2,1)S(1)}, bf16[384,512]{1,0:T(8,128)(2,1)S(1)}, u32[]{:S(2)}, u32[]{:S(2)}) collective-permute-start(bf16[384,512]{1,0:T(8,128)(2,1)S(1)} %collective-permute-done.11.refs_5_), channel_id=1, source_target_pairs={{0,8},{8,16},{16,24},{24,32},{32,40},{40,48},{48,56},{56,0},{1,9},... | collective-permute-start | bytes 1179656 | tf_op jit(solution)/shard_map/ppermute | solution.py:132
